TPU v7x, 32 devices: a whole 2x2x4 slice. The times are simulated.
32 devices in a mesh: seq: 8 (over z, y), ch: 4 (over x, core).
Axes of the slice: x: 2, y: 2, z: 4, core: 2. Of those that a mesh axis runs over, the one named last changes fastest.
Arguments:
- inputs: bfloat16 [256, 4096], P('ch', 'seq'), may hold values from -6 to 6
- cotangent: bfloat16 [256, 4096], P('ch', 'seq'), may hold values from -8 to 8
- w_in: bfloat16 [3, 256, 256], P(None, None, 'ch'), may hold values from -0.375 to 0.375
- short_taps: float32 [3, 3, 256], P(None, None, 'ch'), may hold values from -3 to 3
- filter_one: float32 [256, 4096], P('ch', 'seq'), may hold values from -1 to 1
- filter_two: float32 [256, 4096], P('ch', 'seq'), may hold values from -1 to 1
- w_out: bfloat16 [256, 256], P('ch'), may hold values from -0.375 to 0.375
Outputs:
- inputs_grad: bfloat16 [256, 4096], P('ch', 'seq')
- w_in_grad: float32 [3, 256, 256], P(None, 'seq', 'ch')
- taps_grad: float32 [3, 3, 256], P(None, None, 'ch')
- filter_one_grad: float32 [256, 4096], P('ch', 'seq')
- filter_two_grad: float32 [256, 4096], P('ch', 'seq')
- w_out_grad: float32 [256, 256], P('ch', 'seq')
All inputs are finite; a program needn't handle non-finite values.
Results may differ from a plain program's by a relative error of at most 0.0051.
Values may be sent and summed in bfloat16 or wider, within the bound.
A program may use at most 64 MiB of HBM per device.

v0:
```python
import math

import jax
import jax.numpy as jnp
from jax import lax
from jax.sharding import PartitionSpec as P


def from_behind(array, axis, by):
    devices = lax.axis_size(axis)
    pairs = [(i, i + by) for i in range(devices) if 0 <= i + by < devices]
    return lax.ppermute(array, axis, pairs)


def dense_tables(length):
    index = jnp.arange(length, dtype=jnp.int32)
    angles = 2.0 * math.pi / length * (index[:, None] * index[None, :] % length).astype(jnp.float32)
    return (jnp.cos(angles), jnp.sin(angles))


def coarse_tables(groups):
    freq_index = jnp.arange(2 * groups, dtype=jnp.int32)
    place_index = jnp.arange(groups, dtype=jnp.int32)
    angles = (
        math.pi
        / groups
        * (freq_index[:, None] * place_index[None, :] % (2 * groups)).astype(jnp.float32)
    )
    return (jnp.cos(angles), jnp.sin(angles))


def split_length(length):
    factor = 1
    for candidate in range(1, math.isqrt(length) + 1):
        if length % candidate == 0:
            factor = candidate
    return factor


def twiddle_angles(rows, freq_cols, modulus):
    index = jnp.arange(rows, dtype=jnp.int32)
    product = index[:, None] * freq_cols[None, :] % modulus
    return 2.0 * math.pi / modulus * product.astype(jnp.float32)


def rotate(table_cos, table_sin, real_part, imag_part, orient, pattern):
    cos_real = jnp.einsum(pattern, table_cos, real_part, precision=lax.Precision.HIGHEST)
    cos_imag = jnp.einsum(pattern, table_cos, imag_part, precision=lax.Precision.HIGHEST)
    sin_real = jnp.einsum(pattern, table_sin, real_part, precision=lax.Precision.HIGHEST)
    sin_imag = jnp.einsum(pattern, table_sin, imag_part, precision=lax.Precision.HIGHEST)
    return (cos_real - orient * sin_imag, cos_imag + orient * sin_real)


def factored_dft(real_part, imag_part, orient):
    count, rows, wide = real_part.shape
    first_len = split_length(rows)
    second_len = rows // first_len
    shape = (count, first_len, second_len, wide)
    cos_one, sin_one = dense_tables(first_len)
    real_part, imag_part = rotate(
        cos_one,
        sin_one,
        real_part.reshape(shape),
        imag_part.reshape(shape),
        orient,
        "nj,sjbw->snbw",
    )
    outer = (
        jnp.arange(first_len, dtype=jnp.int32)[:, None]
        * jnp.arange(second_len, dtype=jnp.int32)[None, :]
        % rows
    )
    angles = (2.0 * math.pi / rows * outer.astype(jnp.float32))[None, :, :, None]
    cos_twist = jnp.cos(angles)
    sin_twist = jnp.sin(angles)
    twisted_real = real_part * cos_twist - orient * imag_part * sin_twist
    twisted_imag = imag_part * cos_twist + orient * real_part * sin_twist
    cos_two, sin_two = dense_tables(second_len)
    real_part, imag_part = rotate(
        cos_two, sin_two, twisted_real, twisted_imag, orient, "mb,sabw->smaw"
    )
    return (real_part.reshape(count, rows, wide), imag_part.reshape(count, rows, wide))


def spectral_forward(blocks, freq_cols, modulus):
    rows = blocks.shape[2]
    angles = twiddle_angles(rows, freq_cols, modulus)[None]
    cos_twist = jnp.cos(angles)
    sin_twist = jnp.sin(angles)
    real_part = blocks[:, 0] * cos_twist + blocks[:, 1] * sin_twist
    imag_part = blocks[:, 1] * cos_twist - blocks[:, 0] * sin_twist
    out_real, out_imag = factored_dft(real_part, imag_part, -1.0)
    return jnp.stack([out_real, out_imag], axis=1)


def spectral_inverse(spectra, freq_cols, modulus):
    rows = spectra.shape[2]
    real_part, imag_part = factored_dft(spectra[:, 0], spectra[:, 1], 1.0)
    angles = twiddle_angles(rows, freq_cols, modulus)[None]
    cos_twist = jnp.cos(angles)
    sin_twist = jnp.sin(angles)
    return jnp.stack(
        [
            real_part * cos_twist - imag_part * sin_twist,
            real_part * sin_twist + imag_part * cos_twist,
        ],
        axis=1,
    )


def coarse_forward(table_cos, table_sin, values, pattern):
    real_part = jnp.einsum(pattern, table_cos, values, precision=lax.Precision.HIGHEST)
    imag_part = -jnp.einsum(pattern, table_sin, values, precision=lax.Precision.HIGHEST)
    return jnp.stack([real_part, imag_part], axis=1)


def coarse_inverse(table_cos, table_sin, blocks, modulus):
    real_part = jnp.einsum(
        "pk,sjkc->spjc", table_cos.T, blocks[:, 0], precision=lax.Precision.HIGHEST
    )
    imag_part = jnp.einsum(
        "pk,sjkc->spjc", table_sin.T, blocks[:, 1], precision=lax.Precision.HIGHEST
    )
    return (real_part - imag_part) / modulus


def forward_transform(signals, tables):
    count, rows, chans = signals.shape
    groups = lax.axis_size("seq")
    modulus = 2 * groups * rows
    block = rows // groups
    spread = lax.all_to_all(signals, "seq", split_axis=1, concat_axis=1, tiled=True).reshape(
        count, groups, block, chans
    )
    blocks = coarse_forward(tables[0], tables[1], spread, "kp,spjc->sjkc").reshape(
        count, 2, block, groups, 2 * chans
    )
    blocks = lax.all_to_all(blocks, "seq", split_axis=3, concat_axis=2, tiled=True).reshape(
        count, 2, rows, 2 * chans
    )
    freq_cols = jnp.repeat(2 * lax.axis_index("seq") + jnp.arange(2, dtype=jnp.int32), chans)
    return spectral_forward(blocks, freq_cols, modulus)


def inverse_transform(spectra, tables):
    count, _, rows, wide = spectra.shape
    chans = wide // 2
    groups = lax.axis_size("seq")
    modulus = 2 * groups * rows
    block = rows // groups
    freq_cols = jnp.repeat(2 * lax.axis_index("seq") + jnp.arange(2, dtype=jnp.int32), chans)
    blocks = spectral_inverse(spectra, freq_cols, modulus).reshape(count, 2, rows, 1, wide)
    blocks = lax.all_to_all(blocks, "seq", split_axis=2, concat_axis=3, tiled=True).reshape(
        count, 2, block, 2 * groups, chans
    )
    signals = coarse_inverse(tables[0], tables[1], blocks, modulus)
    return lax.all_to_all(signals, "seq", split_axis=1, concat_axis=2, tiled=True).reshape(
        count, rows, chans
    )


def complex_product(left, right, conjugate):
    left_real = left[:, 0]
    left_imag = -left[:, 1] if conjugate else left[:, 1]
    return jnp.stack(
        [
            left_real * right[:, 0] - left_imag * right[:, 1],
            left_real * right[:, 1] + left_imag * right[:, 0],
        ],
        axis=1,
    )


def local(inputs, cotangent, w_in, short_taps, filter_one, filter_two, w_out):
    chans, rows = inputs.shape
    groups = lax.axis_size("seq")
    width = chans * lax.axis_size("ch")
    scale = 1.0 / math.sqrt(rows * groups)
    seq_cos, seq_sin = coarse_tables(groups)
    tables = (seq_cos, seq_sin)
    inputs_cols, cotangent_cols = (
        lax.all_gather(inputs, "ch", axis=0, tiled=True),
        lax.all_gather(cotangent, "ch", axis=0, tiled=True),
    )
    inputs_full = inputs_cols.T
    cotangent_full = cotangent_cols.T
    filter_first = filter_one.T
    filter_second = filter_two.T
    w_joined = w_in.transpose(1, 0, 2).reshape(width, 3 * chans)
    projected = jnp.dot(inputs_full, w_joined, preferred_element_type=jnp.float32)
    taps = short_taps.transpose(1, 0, 2).reshape(3, 3 * chans)
    before = from_behind(projected[rows - 2 :], "seq", 1)
    padded = jnp.concatenate([before, projected], axis=0)
    filtered = taps[0] * projected + taps[1] * padded[1 : rows + 1] + taps[2] * padded[:rows]
    gate_one = filtered[:, :chans]
    gate_two = filtered[:, chans : 2 * chans]
    value = filtered[:, 2 * chans :]
    spectra = forward_transform(jnp.stack([filter_first, value, filter_second]), tables)
    spec_two = spectra[2:3]
    spec_one = spectra[0:1]
    spec_value = spectra[1:2]
    first = inverse_transform(complex_product(spec_one, spec_value, False), tables)[0]
    inner = gate_one * first
    spec_inner = forward_transform(inner[None], tables)
    second = inverse_transform(complex_product(spec_inner, spec_two, False), tables)[0]
    gated = (gate_two * second).astype(jnp.bfloat16)
    out_terms = (
        lax.dot_general(
            gated, cotangent_full, (((0,), (0,)), ((), ())), preferred_element_type=jnp.float32
        )
        * scale
    )
    w_out_grad = lax.psum_scatter(out_terms, "seq", scatter_dimension=1, tiled=True)
    gated_grad = lax.dot_general(
        cotangent_full, w_out, (((1,), (1,)), ((), ())), preferred_element_type=jnp.float32
    )
    gate_two_grad = gated_grad * second
    second_grad = gated_grad * gate_two
    spec_second = forward_transform(second_grad[None], tables)
    back_two = inverse_transform(
        jnp.concatenate(
            [
                complex_product(spec_two, spec_second, True),
                complex_product(spec_inner, spec_second, True),
            ],
            axis=0,
        ),
        tables,
    )
    inner_grad = back_two[0]
    filter_two_grad = back_two[1] * scale
    gate_one_grad = inner_grad * first
    first_grad = inner_grad * gate_one
    spec_first = forward_transform(first_grad[None], tables)
    back_one = inverse_transform(
        jnp.concatenate(
            [
                complex_product(spec_one, spec_first, True),
                complex_product(spec_value, spec_first, True),
            ],
            axis=0,
        ),
        tables,
    )
    value_grad = back_one[0]
    filter_one_grad = back_one[1] * scale
    filtered_grad = jnp.concatenate([gate_one_grad, gate_two_grad, value_grad], axis=1)
    after = from_behind(filtered_grad[:2], "seq", -1)
    extended = jnp.concatenate([filtered_grad, after], axis=0)
    tap_terms = (
        jnp.stack(
            [
                jnp.sum(filtered_grad * projected, axis=0),
                jnp.sum(filtered_grad * padded[1 : rows + 1], axis=0),
                jnp.sum(filtered_grad * padded[:rows], axis=0),
            ]
        )
        * scale
    )
    taps_grad = lax.psum(tap_terms, "seq").reshape(3, 3, chans).transpose(1, 0, 2)
    projected_grad = (
        taps[0] * filtered_grad
        + taps[1] * extended[1 : rows + 1]
        + taps[2] * extended[2 : rows + 2]
    ).astype(jnp.bfloat16)
    in_terms = jnp.dot(inputs_cols, projected_grad, preferred_element_type=jnp.float32) * scale
    in_terms = in_terms.reshape(width, 3, chans).transpose(1, 0, 2)
    w_in_grad = lax.psum_scatter(in_terms, "seq", scatter_dimension=1, tiled=True)
    input_terms = lax.dot_general(
        w_joined, projected_grad, (((1,), (1,)), ((), ())), preferred_element_type=jnp.float32
    )
    inputs_grad = lax.psum_scatter(input_terms, "ch", scatter_dimension=0, tiled=True).astype(
        jnp.bfloat16
    )
    return (inputs_grad, w_in_grad, taps_grad, filter_one_grad.T, filter_two_grad.T, w_out_grad)


def solution(mesh):
    in_specs = (
        P("ch", "seq"),
        P("ch", "seq"),
        P(None, None, "ch"),
        P(None, None, "ch"),
        P("ch", "seq"),
        P("ch", "seq"),
        P("ch", None),
    )
    out_specs = (
        P("ch", "seq"),
        P(None, "seq", "ch"),
        P(None, None, "ch"),
        P("ch", "seq"),
        P("ch", "seq"),
        P("ch", "seq"),
    )
    return jax.shard_map(local, mesh=mesh, in_specs=in_specs, out_specs=out_specs, check_vma=False)
```

profile of v0, /device:TPU:0, one launch (start us, length us, event | category | flops | bytes accessed | tf_op | source)
XLA Modules:
  0.0 542.4 jit_solution(10118559438007432740)
XLA Ops:
  7.2 7.5 %all_gather.6 = bf16[256,512]{1,0:T(8,128)(2,1)S(1)} all-gather(bf16[64,512]{1,0:T(8,128)(2,1)} %param.7), channel_id=1, replica_groups=mesh['seq'=8,'ch'=4] {'ch'}, dimensions={0}, use_global_device_ids=true | all-gather | bytes 327680 | tf_op jit(solution)/shard_map/all_gather | solution.py:182
  19.2 6.0 %all_gather.7 = bf16[256,512]{1,0:T(8,128)(2,1)S(1)} all-gather(bf16[64,512]{1,0:T(8,128)(2,1)} %param.8), channel_id=1, replica_groups=mesh['seq'=8,'ch'=4] {'ch'}, dimensions={0}, use_global_device_ids=true | all-gather | bytes 327680 | tf_op jit(solution)/shard_map/all_gather | solution.py:183
  30.4 4.9 all-to-all-start.2
  37.3 5.5 %all-to-all-done.2 = f32[8,1,4096]{2,1,0:T(1,128)S(1)} async-done(((f32[8,1,4096]{2,1,0:T(1,128)}), f32[8,1,4096]{2,1,0:T(1,128)S(1)}, u32[]{:S(2)}, u32[]{:S(2)}) %all-to-all-start.2) | async-done | bytes 131104 | tf_op jit(solution)/shard_map/all_to_all | solution.py:132
  50.2 6.9 %all-to-all-done = f32[8,1,12288]{2,1,0:T(1,128)S(1)} async-done(((f32[8,1,12288]{2,1,0:T(1,128)}), f32[8,1,12288]{2,1,0:T(1,128)S(1)}, u32[]{:S(2)}, u32[]{:S(2)}) %all-to-all-start) | async-done | bytes 393248 | tf_op jit(solution)/shard_map/all_to_all | solution.py:132
  57.1 4.7 all-to-all-start.3
  69.7 5.6 %all-to-all-done.3 = f32[1,2,64,8,128]{4,2,1,0,3:T(8,128)} async-done(((f32[1,2,64,8,128]{4,2,1,0,3:T(8,128)}), f32[1,2,64,8,128]{4,2,1,0,3:T(8,128)}, u32[]{:S(2)}, u32[]{:S(2)}) %all-to-all-start.3) | async-done | bytes 524320 | tf_op jit(solution)/shard_map/all_to_all | solution.py:138
  75.3 3.7 all-to-all-start.1
  85.6 29.7 %all-to-all-done.1 = f32[3,2,64,8,128]{4,2,1,0,3:T(8,128)S(1)} async-done(((f32[3,2,64,8,128]{4,2,1,0,3:T(8,128)}), f32[3,2,64,8,128]{4,2,1,0,3:T(8,128)S(1)}, u32[]{:S(2)}, u32[]{:S(2)}) %all-to-all-start.1) | async-done | bytes 1572896 | tf_op jit(solution)/shard_map/all_to_all | solution.py:138
  133.5 18.0 %all_to_all.176 = f32[1,2,512,1,128]{4,1,3,0,2:T(2,128)S(1)} all-to-all(f32[1,2,512,1,128]{4,1,3,0,2:T(2,128)S(1)} %copy.343), channel_id=1, replica_groups=mesh['seq'=8,'ch'=4] {'seq'}, dimensions={2} | all-to-all | bytes 1048576 | tf_op jit(solution)/shard_map/all_to_all | solution.py:153
  153.2 10.8 %all_to_all.177 = f32[8,1,4096]{2,1,0:T(1,128)S(1)} all-to-all(f32[8,1,4096]{2,1,0:T(1,128)S(1)} %reshape.1738), channel_id=1, replica_groups=mesh['seq'=8,'ch'=4] {'seq'}, dimensions={0} | all-to-all | bytes 262144 | tf_op jit(solution)/shard_map/all_to_all | solution.py:157
  167.8 9.7 %all_to_all.178 = f32[8,1,4096]{2,1,0:T(1,128)S(1)} all-to-all(f32[8,1,4096]{2,1,0:T(1,128)S(1)} %reshape.1740), channel_id=1, replica_groups=mesh['seq'=8,'ch'=4] {'seq'}, dimensions={0} | all-to-all | bytes 262144 | tf_op jit(solution)/shard_map/all_to_all | solution.py:132
  186.4 10.4 %all-to-all-done.7 = f32[1,2,64,8,128]{4,2,1,0,3:T(8,128)S(1)} async-done(((f32[1,2,64,8,128]{4,2,1,0,3:T(8,128)}), f32[1,2,64,8,128]{4,2,1,0,3:T(8,128)S(1)}, u32[]{:S(2)}, u32[]{:S(2)}) %all-to-all-start.7) | async-done | bytes 524320 | tf_op jit(solution)/shard_map/all_to_all | solution.py:138
  212.5 28.0 %all_to_all.179 = f32[2,2,512,1,128]{4,0,1,3,2:T(2,128)S(1)} all-to-all(f32[2,2,512,1,128]{4,0,1,3,2:T(2,128)S(1)} %copy.375), channel_id=1, replica_groups=mesh['seq'=8,'ch'=4] {'seq'}, dimensions={2} | all-to-all | bytes 2097152 | tf_op jit(solution)/shard_map/all_to_all | solution.py:153
  243.4 12.0 %all_to_all.180 = f32[8,1,8192]{2,1,0:T(1,128)S(1)} all-to-all(f32[8,1,8192]{2,1,0:T(1,128)S(1)} %reshape.1742), channel_id=1, replica_groups=mesh['seq'=8,'ch'=4] {'seq'}, dimensions={0} | all-to-all | bytes 524288 | tf_op jit(solution)/shard_map/all_to_all | solution.py:157
  261.0 10.6 %all_to_all.181 = f32[8,1,4096]{2,1,0:T(1,128)S(1)} all-to-all(f32[8,1,4096]{2,1,0:T(1,128)S(1)} %reshape.1744), channel_id=1, replica_groups=mesh['seq'=8,'ch'=4] {'seq'}, dimensions={0} | all-to-all | bytes 262144 | tf_op jit(solution)/shard_map/all_to_all | solution.py:132
  274.8 15.7 %all_to_all.182 = f32[1,2,64,8,128]{4,2,1,0,3:T(8,128)S(1)} all-to-all(f32[1,2,64,8,128]{4,2,1,0,3:T(8,128)S(1)} %pad_maximum_fusion.3), channel_id=1, replica_groups=mesh['seq'=8,'ch'=4] {'seq'}, dimensions={3} | all-to-all | bytes 1048576 | tf_op jit(solution)/shard_map/all_to_all | solution.py:138
  304.8 3.8 all-to-all-start.10
  328.4 22.9 %all-to-all-done.14 = f32[2,2,512,1,128]{4,0,1,3,2:T(2,128)S(1)} async-done(((f32[2,2,512,1,128]{4,0,1,3,2:T(2,128)}), f32[2,2,512,1,128]{4,0,1,3,2:T(2,128)S(1)}, u32[]{:S(2)}, u32[]{:S(2)}) %all-to-all-start.14) | async-done | bytes 1048608 | tf_op jit(solution)/shard_map/all_to_all | solution.py:153
  366.9 6.9 %all-to-all-done.15 = f32[8,1,8192]{2,1,0:T(1,128)S(1)} async-done(((f32[8,1,8192]{2,1,0:T(1,128)}), f32[8,1,8192]{2,1,0:T(1,128)S(1)}, u32[]{:S(2)}, u32[]{:S(2)}) %all-to-all-start.15) | async-done | bytes 262176 | tf_op jit(solution)/shard_map/all_to_all | solution.py:157
  376.9 5.2 collective-permute-done.1
  389.1 19.6 %psum.7 = f32[3,3,64]{2,0,1:T(4,128)S(1)} all-reduce(f32[3,3,64]{2,0,1:T(4,128)S(1)} %bitcast.710), channel_id=1, replica_groups=mesh['seq'=8,'ch'=4] {'seq'}, use_global_device_ids=true, to_apply=%region_5.6 | all-reduce | flops 576 | bytes 4608 | tf_op jit(solution)/shard_map/psum | solution.py:260
  411.1 59.1 %reduce-scatter.8.cloned.1.call-done = f32[64,32]{0,1:T(8,128)} async-done(((f32[64,256]{0,1:T(8,128)}), f32[64,32]{0,1:T(8,128)}) %reduce-scatter.8.cloned.1.call-update) | async-done | bytes 8208 | tf_op jit(solution)/shard_map/reduce_scatter | solution.py:213
  470.2 65.4 %reduce-scatter.6.cloned.1.call-done = f32[3,32,64]{2,1,0:T(8,128)} async-done(((f32[3,256,64]{2,1,0:T(8,128)}), f32[3,32,64]{2,1,0:T(8,128)}) %reduce-scatter.6.cloned.1.call-update) | async-done | bytes 24592 | tf_op jit(solution)/shard_map/reduce_scatter | solution.py:268
  (333 shorter events, 153.7 us)
Async XLA Ops:
  7.2 18.7 %copy-start.29 = (bf16[64,256]{1,0:T(8,128)(2,1)S(1)}, bf16[64,256]{1,0:T(8,128)(2,1)}, u32[]{:S(2)}) copy-start(bf16[64,256]{1,0:T(8,128)(2,1)} %param.13) | copy-start | bytes 98308
  7.2 18.9 %copy-start.38 = (f32[3,3,64]{2,1,0:T(4,128)S(1)}, f32[3,3,64]{2,1,0:T(4,128)}, u32[]{:S(2)}) copy-start(f32[3,3,64]{2,1,0:T(4,128)} %param.10) | copy-start | bytes 6916
  15.6 13.9 %copy-start.1 = (f32[512,192]{0,1:T(8,128)}, f32[512,192]{0,1:T(8,128)S(1)}, u32[]{:S(2)}) copy-start(f32[512,192]{0,1:T(8,128)S(1)} %fusion.731) | copy-start | bytes 1179652
  15.7 10.7 %collective-permute-start = (f32[2,192]{0,1:T(8,128)S(1)}, f32[2,192]{0,1:T(8,128)S(1)}, u32[]{:S(2)}, u32[]{:S(2)}) collective-permute-start(f32[2,192]{0,1:T(8,128)S(1)} %slice.223), channel_id=1, source_target_pairs={{0,4},{4,8},{8,12},{12,16},{16,20},{20,24},{24,28},{1,5},{5,9},{9,... | collective-permute-start | bytes 4616 | tf_op jit(solution)/shard_map/ppermute | solution.py:12
  30.4 12.4 %all-to-all-start.2 = ((f32[8,1,4096]{2,1,0:T(1,128)}), f32[8,1,4096]{2,1,0:T(1,128)S(1)}, u32[]{:S(2)}, u32[]{:S(2)}) async-start(f32[8,1,4096]{2,1,0:T(1,128)} %reshape.1734), calls=%async_computation.2 | async-start | bytes 262144 | tf_op jit(solution)/shard_map/all_to_all | solution.py:132
  42.8 14.3 %all-to-all-start = ((f32[8,1,12288]{2,1,0:T(1,128)}), f32[8,1,12288]{2,1,0:T(1,128)S(1)}, u32[]{:S(2)}, u32[]{:S(2)}) async-start(f32[8,1,12288]{2,1,0:T(1,128)} %reshape.1736), calls=%async_computation | async-start | bytes 786432 | tf_op jit(solution)/shard_map/all_to_all | solution.py:132
  57.1 18.2 %all-to-all-start.3 = ((f32[1,2,64,8,128]{4,2,1,0,3:T(8,128)}), f32[1,2,64,8,128]{4,2,1,0,3:T(8,128)}, u32[]{:S(2)}, u32[]{:S(2)}) async-start(f32[1,2,64,8,128]{4,2,1,0,3:T(8,128)} %pad_maximum_fusion.1), calls=%async_computation.3 | async-start | bytes 1048576 | tf_op jit(solution)/shard_map/all_to_all | solution.py:138
  75.3 40.0 %all-to-all-start.1 = ((f32[3,2,64,8,128]{4,2,1,0,3:T(8,128)}), f32[3,2,64,8,128]{4,2,1,0,3:T(8,128)S(1)}, u32[]{:S(2)}, u32[]{:S(2)}) async-start(f32[3,2,64,8,128]{4,2,1,0,3:T(8,128)} %pad_maximum_fusion), calls=%async_computation.1 | async-start | bytes 3145728 | tf_op jit(solution)/shard_map/all_to_all | solution.py:138
  79.2 117.7 %copy-start.30 = (s32[128]{0:T(128)}, s32[128]{0:T(128)S(1)}, u32[]{:S(2)}) copy-start(s32[128]{0:T(128)S(1)} %mul.2432) | copy-start | bytes 1540
  165.2 14.3 %copy-start.15 = (f32[512,64]{0,1:T(8,128)}, f32[512,64]{0,1:T(8,128)S(1)}, u32[]{:S(2)}) copy-start(f32[512,64]{0,1:T(8,128)S(1)} %copy.448) | copy-start | bytes 393220
  181.5 15.3 %all-to-all-start.7 = ((f32[1,2,64,8,128]{4,2,1,0,3:T(8,128)}), f32[1,2,64,8,128]{4,2,1,0,3:T(8,128)S(1)}, u32[]{:S(2)}, u32[]{:S(2)}) async-start(f32[1,2,64,8,128]{4,2,1,0,3:T(8,128)} %pad_maximum_fusion.2), calls=%async_computation.7 | async-start | bytes 1048576 | tf_op jit(solution)/shard_map/all_to_all | solution.py:138
  186.0 25.3 %copy-start.4 = (f32[512,128]{1,0:T(8,128)}, f32[512,128]{1,0:T(8,128)S(1)}, u32[]{:S(2)}) copy-start(f32[512,128]{1,0:T(8,128)S(1)} %get-tuple-element.108) | copy-start | bytes 786436
  186.1 10.8 %copy-start.25 = (s32[16,32]{1,0:T(8,128)S(1)}, s32[16,32]{1,0:T(8,128)}, u32[]{:S(2)}) copy-start(s32[16,32]{1,0:T(8,128)} %copy-done.24) | copy-start | bytes 6148
  243.4 14.4 %copy-start.16 = (f32[512,64]{0,1:T(8,128)S(1)}, f32[512,64]{0,1:T(8,128)}, u32[]{:S(2)}) copy-start(f32[512,64]{0,1:T(8,128)} %copy-done.15) | copy-start | bytes 393220
  274.8 15.8 %copy-start.26 = (s32[16,32]{1,0:T(8,128)S(1)}, s32[16,32]{1,0:T(8,128)}, u32[]{:S(2)}) copy-start(s32[16,32]{1,0:T(8,128)} %copy-done.24) | copy-start | bytes 6148
  274.8 15.8 %copy-start.31 = (s32[128]{0:T(128)S(1)}, s32[128]{0:T(128)}, u32[]{:S(2)}) copy-start(s32[128]{0:T(128)} %copy-done.30) | copy-start | bytes 1540
  304.8 17.6 %all-to-all-start.10 = ((f32[1,2,512,1,128]{4,1,3,0,2:T(2,128)}), f32[1,2,512,1,128]{4,1,3,0,2:T(2,128)S(1)}, u32[]{:S(2)}, u32[]{:S(2)}) async-start(f32[1,2,512,1,128]{4,1,3,0,2:T(2,128)} %copy.392), calls=%async_computation.10 | async-start | bytes 1048576 | tf_op jit(solution)/shard_map/all_to_all | solution.py:153
  322.4 28.9 %all-to-all-start.14 = ((f32[2,2,512,1,128]{4,0,1,3,2:T(2,128)}), f32[2,2,512,1,128]{4,0,1,3,2:T(2,128)S(1)}, u32[]{:S(2)}, u32[]{:S(2)}) async-start(f32[2,2,512,1,128]{4,0,1,3,2:T(2,128)} %copy.426), calls=%async_computation.14 | async-start | bytes 2097152 | tf_op jit(solution)/shard_map/all_to_all | solution.py:153
  351.3 10.9 %all-to-all-start.11 = ((f32[8,1,4096]{2,1,0:T(1,128)}), f32[8,1,4096]{2,1,0:T(1,128)S(1)}, u32[]{:S(2)}, u32[]{:S(2)}) async-start(f32[8,1,4096]{2,1,0:T(1,128)} %reshape.1748), calls=%async_computation.11 | async-start | bytes 262144 | tf_op jit(solution)/shard_map/all_to_all | solution.py:157
  362.2 11.6 %all-to-all-start.15 = ((f32[8,1,8192]{2,1,0:T(1,128)}), f32[8,1,8192]{2,1,0:T(1,128)S(1)}, u32[]{:S(2)}, u32[]{:S(2)}) async-start(f32[8,1,8192]{2,1,0:T(1,128)} %reshape.1746), calls=%async_computation.15 | async-start | bytes 524288 | tf_op jit(solution)/shard_map/all_to_all | solution.py:157
  365.7 43.6 %reduce-scatter.10.cloned.1.call-start = ((), (), s32[]{:S(2)}) async-start(), calls=%async_computation.21 | async-start | bytes 655360
  375.6 6.5 %collective-permute-start.1 = (f32[2,192]{0,1:T(8,128)S(1)}, f32[2,192]{0,1:T(8,128)S(1)}, u32[]{:S(2)}, u32[]{:S(2)}) collective-permute-start(f32[2,192]{0,1:T(8,128)S(1)} %slice.258), channel_id=1, source_target_pairs={{4,0},{8,4},{12,8},{16,12},{20,16},{24,20},{28,24},{5,1},{9,5},{13... | collective-permute-start | bytes 4616 | tf_op jit(solution)/shard_map/ppermute | solution.py:12
  384.3 85.9 %reduce-scatter.8.cloned.1.call-start = ((), (), s32[]{:S(2)}) async-start(), calls=%async_computation.20 | async-start | bytes 147456 | tf_op jit(solution)/shard_map/reduce_scatter | solution.py:213
  386.2 149.5 %reduce-scatter.6.cloned.1.call-start = ((), (), s32[]{:S(2)}) async-start(), calls=%async_computation.19 | async-start | bytes 442368 | tf_op jit(solution)/shard_map/reduce_scatter | solution.py:268
  (29 other events, 136.3 us)
Sparse Core Ops, SparseCore 0:
  384.4 20.5 reduce-scatter.9
  409.3 60.8 reduce-scatter.7
  474.4 61.1 reduce-scatter.5
where the time goes:
time: 549 us; the launch traced here: 542 us
  waiting for transfers between devices  225 us (41%)
  blocking collectives  138 us (25%)
  matrix products  62.2 us (11%)
  starting transfers between devices  39.6 us (7%)
  local copies, waits for them, and re-layouts  33 us (6%)
  other arithmetic  28.8 us (5%)
  between operations  16 us (3%)
    reduce_scatter x1, waiting for transfers between devices, local(): lax.psum_scatter(in_terms, 'seq', scatter_dimension=1, tiled=True)  65.4 us
    reduce_scatter x1, waiting for transfers between devices, local(): lax.psum_scatter(out_terms, 'seq', scatter_dimension=1, tiled=True)  59.1 us
    all_to_all x2, blocking collectives, inverse_transform(): lax.all_to_all(blocks, 'seq', split_axis=2, concat_axis=3, tiled=True)  46 us
    all_to_all x3, waiting for transfers between devices, forward_transform(): lax.all_to_all(blocks, 'seq', split_axis=3, concat_axis=2, tiled=True)  45.6 us
    all_to_all x2, waiting for transfers between devices, inverse_transform(): lax.all_to_all(blocks, 'seq', split_axis=2, concat_axis=3, tiled=True)  26.4 us
    all_to_all x2, blocking collectives, inverse_transform(): lax.all_to_all(signals, 'seq', split_axis=1, concat_axis=2, tiled=True)  22.8 us
    all_to_all x2, blocking collectives, forward_transform(): lax.all_to_all(signals, 'seq', split_axis=1, concat_axis=1, tiled=True)  20.4 us
    psum x1, blocking collectives, local(): lax.psum(tap_terms, 'seq').reshape(3, 3, chans).transpose(1, 0, 2)  19.6 us
  transfers between devices with their start and end apart: 14, of which 12 were waited for; matrix products, arithmetic and copies ran while one was open for 9% of the time, Pallas kernels for 0%

commit v1 on v0

v1 whole, which is shorter than its diff:
```python
import functools
import math

import jax
import jax.numpy as jnp
import ml_dtypes
import numpy as np
from jax import lax
from jax.experimental import pallas as pl
from jax.experimental.pallas import tpu as pltpu
from jax.sharding import PartitionSpec as P

LANES = 128
MESH = pl.DeviceIdType.MESH
BF16 = jnp.bfloat16
F32 = jnp.float32


def halves(table):
    high = table.astype(np.float32).astype(ml_dtypes.bfloat16)
    low = (table - high.astype(np.float64)).astype(np.float32).astype(ml_dtypes.bfloat16)
    return [high, low]


def dft_tables(tokens, chans):
    blocks = tokens // LANES
    size = 2 * tokens
    eye = np.eye(chans)
    place = np.arange(blocks, dtype=np.float64)
    half = np.arange(blocks, dtype=np.float64) + 0.5
    coarse = 2.0 * np.pi / (2 * blocks) * np.outer(half, place)
    cos_one, sin_one = np.cos(coarse), np.sin(coarse)
    forward_one = np.concatenate([np.kron(cos_one, eye), -np.kron(sin_one, eye)], axis=0)
    inverse_one = 2.0 / size * np.concatenate(
        [np.kron(cos_one.T, eye), -np.kron(sin_one.T, eye)], axis=1
    )
    lane = np.arange(LANES)
    fine = 2.0 * np.pi / LANES * (np.outer(lane, lane) % LANES)
    cos_two, sin_two = np.cos(fine), np.sin(fine)
    forward_two = np.block([[cos_two, -sin_two], [sin_two, cos_two]])
    inverse_two = np.block([[cos_two, sin_two], [-sin_two, cos_two]])
    twist = np.repeat(2.0 * np.pi / size * np.outer(half, lane), chans, axis=0)
    tables = halves(forward_one) + halves(inverse_one) + halves(forward_two) + halves(inverse_two)
    return tables + [np.cos(twist).astype(np.float32), np.sin(twist).astype(np.float32)]


def split(value):
    high = value.astype(BF16)
    return high, (value - high.astype(F32)).astype(BF16)


def dot(left, right):
    return jnp.dot(left, right, preferred_element_type=F32)


def dot_rows(left, right):
    return lax.dot_general(left, right, (((1,), (1,)), ((), ())), preferred_element_type=F32)


def kernel(
    seqs,
    groups,
    x_ref,
    g_ref,
    f1_ref,
    f2_ref,
    wt_ref,
    wj_ref,
    wo_ref,
    taps_ref,
    mf_hi,
    mf_lo,
    mi_hi,
    mi_lo,
    df_hi,
    df_lo,
    di_hi,
    di_lo,
    tc_ref,
    ts_ref,
    dx_ref,
    dw_ref,
    dt_ref,
    df1_ref,
    df2_ref,
    xg,
    filt_out,
    filt_in,
    sig_out,
    sig_in,
    gated_out,
    gated_in,
    fg_out,
    fg_in,
    pg_out,
    pg_in,
    grads,
    w_out_buf,
    w_in_buf,
    dx_out,
    dx_in,
    sems_x,
    sems_seq,
    sems_dx,
):
    chans, span = x_ref.shape
    own = chans // seqs
    parts = span // LANES
    piece = parts * own
    rows = piece * seqs
    width = chans * groups
    scale = 1.0 / math.sqrt(span * seqs)
    me = lax.axis_index("seq")
    mine = lax.axis_index("ch")

    barrier = pltpu.get_barrier_semaphore()
    for k in range(1, seqs):
        pl.semaphore_signal(
            barrier, inc=1, device_id=(lax.rem(me + k, seqs), mine), device_id_type=MESH
        )
    for k in range(1, groups):
        pl.semaphore_signal(
            barrier, inc=1, device_id=(me, lax.rem(mine + k, groups)), device_id_type=MESH
        )

    def fold(value, first, target, index):
        for q in range(parts):
            target[index + (pl.ds(q * own, own), slice(None))] = value[
                first : first + own, q * LANES : (q + 1) * LANES
            ]

    for j in range(seqs):
        fold(f1_ref[pl.ds(j * own, own), :], 0, filt_out, (j, 0))
        fold(f2_ref[pl.ds(j * own, own), :], 0, filt_out, (j, 1))

    pl.semaphore_wait(barrier, seqs - 1 + groups - 1)

    def remote(source, target, send_sem, recv_sem, device):
        copy = pltpu.make_async_remote_copy(
            src_ref=source,
            dst_ref=target,
            send_sem=send_sem,
            recv_sem=recv_sem,
            device_id=device,
            device_id_type=MESH,
        )
        copy.start()
        return copy

    x_copies = []
    for k in range(1, groups):
        peer = (me, lax.rem(mine + k, groups))
        for a, ref in enumerate((x_ref, g_ref)):
            x_copies.append(
                remote(ref, xg.at[a, mine], sems_x.at[0, a, k], sems_x.at[1, a, k], peer)
            )

    def exchange(out, into, kind):
        copies = []
        for k in range(1, seqs):
            to = lax.rem(me + k, seqs)
            copies.append(
                remote(
                    out.at[to], into.at[me], sems_seq.at[0, kind, k], sems_seq.at[1, kind, k], (to, mine)
                )
            )
        into[me] = out[me]
        return copies

    def finish(copies):
        for copy in copies:
            copy.wait()

    filt_copies = exchange(filt_out, filt_in, 0)
    xg[0, mine] = x_ref[...]
    xg[1, mine] = g_ref[...]
    finish(x_copies)
    x_all = xg[0].reshape(width, span)
    g_all = xg[1].reshape(width, span)
    projected = dot(wt_ref[...], x_all)
    gated_grad_here = dot(wo_ref[...], g_all)
    for j in range(seqs):
        for i in range(3):
            fold(projected, i * chans + j * own, sig_out, (j, i))
        fold(gated_grad_here, j * own, sig_out, (j, 3))
    sig_copies = exchange(sig_out, sig_in, 1)

    cos_twist = tc_ref[...]
    sin_twist = ts_ref[...]

    def left(table_hi, table_lo, value):
        high, low = split(value)
        return dot(table_hi[...], high) + dot(table_hi[...], low) + dot(table_lo[...], high)

    def right(value, table_hi, table_lo):
        high, low = split(value)
        return dot(high, table_hi[...]) + dot(low, table_hi[...]) + dot(high, table_lo[...])

    def forward(signals):
        joined = signals[0] if len(signals) == 1 else jnp.concatenate(signals, axis=1)
        coarse = left(mf_hi, mf_lo, joined)
        out = []
        for s in range(len(signals)):
            real = coarse[:rows, s * LANES : (s + 1) * LANES]
            imag = coarse[rows:, s * LANES : (s + 1) * LANES]
            turned = jnp.concatenate(
                [
                    real * cos_twist + imag * sin_twist,
                    imag * cos_twist - real * sin_twist,
                ],
                axis=1,
            )
            spectrum = right(turned, df_hi, df_lo)
            out.append((spectrum[:, :LANES], spectrum[:, LANES:]))
        return out

    def inverse(spectra):
        turned = []
        for real, imag in spectra:
            fine = right(jnp.concatenate([real, imag], axis=1), di_hi, di_lo)
            real, imag = fine[:, :LANES], fine[:, LANES:]
            turned.append(
                jnp.concatenate(
                    [
                        real * cos_twist - imag * sin_twist,
                        real * sin_twist + imag * cos_twist,
                    ],
                    axis=0,
                )
            )
        joined = turned[0] if len(turned) == 1 else jnp.concatenate(turned, axis=1)
        result = left(mi_hi, mi_lo, joined)
        return [result[:, s * LANES : (s + 1) * LANES] for s in range(len(spectra))]

    def times(a, b):
        return (a[0] * b[0] - a[1] * b[1], a[0] * b[1] + a[1] * b[0])

    def conj_times(a, b):
        return (a[0] * b[0] + a[1] * b[1], a[0] * b[1] - a[1] * b[0])

    finish(filt_copies)
    spec_one, spec_two = forward(
        [filt_in[:, 0].reshape(rows, LANES), filt_in[:, 1].reshape(rows, LANES)]
    )

    row = lax.broadcasted_iota(jnp.int32, (rows, LANES), 0)
    lane = lax.broadcasted_iota(jnp.int32, (rows, LANES), 1)

    def delayed(value, k):
        rolled = pltpu.roll(value, k, 1)
        before = jnp.where(row < own, 0.0, pltpu.roll(rolled, own, 0))
        return jnp.where(lane < k, before, rolled)

    def advanced(value, k):
        rolled = pltpu.roll(value, LANES - k, 1)
        after = jnp.where(row >= rows - own, 0.0, pltpu.roll(rolled, rows - own, 0))
        return jnp.where(lane >= LANES - k, after, rolled)

    def tap(i, k):
        tile = taps_ref[3 * i + k]
        return jnp.broadcast_to(tile[None], (rows // 8, 8, LANES)).reshape(rows, LANES)

    finish(sig_copies)

    def projection(i):
        value = sig_in[:, i].reshape(rows, LANES)
        return value, delayed(value, 1), delayed(value, 2)

    def filtered(i):
        now, one, two = projection(i)
        return tap(i, 0) * now + tap(i, 1) * one + tap(i, 2) * two

    gate_one = filtered(0)
    gate_two = filtered(1)
    value = filtered(2)
    gated_grad = sig_in[:, 3].reshape(rows, LANES)

    second_grad = gated_grad * gate_two
    spec_value, spec_second = forward([value, second_grad])
    (first, inner_grad) = inverse([times(spec_one, spec_value), conj_times(spec_two, spec_second)])
    inner = gate_one * first
    gate_one_grad = inner_grad * first
    first_grad = inner_grad * gate_one
    spec_inner, spec_first = forward([inner, first_grad])
    second, filter_two_grad = inverse(
        [times(spec_inner, spec_two), conj_times(spec_inner, spec_second)]
    )
    gated = gate_two * second
    gated_out[...] = gated.reshape(seqs, piece, LANES).astype(BF16)
    gated_copies = exchange(gated_out, gated_in, 2)
    value_grad, filter_one_grad = inverse(
        [conj_times(spec_one, spec_first), conj_times(spec_value, spec_first)]
    )
    gate_two_grad = gated_grad * second

    for i, grad in enumerate((gate_one_grad, gate_two_grad, value_grad)):
        back = tap(i, 0) * grad + tap(i, 1) * advanced(grad, 1) + tap(i, 2) * advanced(grad, 2)
        pg_out[:, i] = back.reshape(seqs, piece, LANES).astype(BF16)
    pg_copies = exchange(pg_out, pg_in, 3)
    fg_out[:, 0] = (filter_one_grad * scale).reshape(seqs, piece, LANES)
    fg_out[:, 1] = (filter_two_grad * scale).reshape(seqs, piece, LANES)
    fg_copies = exchange(fg_out, fg_in, 4)

    small_lane = lax.broadcasted_iota(jnp.int32, (8, LANES), 1)
    tap_terms = jnp.zeros((8, LANES), F32)
    for i, grad in enumerate((gate_one_grad, gate_two_grad, value_grad)):
        for k, shifted in enumerate(projection(i)):
            total = jnp.sum((grad * shifted).reshape(rows // 8, 8, LANES), axis=0)
            total = jnp.sum(total, axis=1, keepdims=True) * scale
            tap_terms = jnp.where(small_lane == 3 * i + k, total, tap_terms)
    dt_ref[me] = tap_terms
    tap_copies = []
    for k in range(1, seqs):
        to = lax.rem(me + k, seqs)
        tap_copies.append(
            remote(
                dt_ref.at[me], dt_ref.at[me], sems_seq.at[0, 5, k], sems_seq.at[1, 5, k], (to, mine)
            )
        )

    def unfold(value, first, source, target):
        for q in range(parts):
            target[pl.ds(first + source * own, own), q * LANES : (q + 1) * LANES] = value[
                q * own : (q + 1) * own, :
            ]

    finish(gated_copies)
    for j in range(seqs):
        unfold(gated_in[j].astype(F32), 3 * chans, j, grads)
    finish(pg_copies)
    for j in range(seqs):
        for i in range(3):
            unfold(pg_in[j, i].astype(F32), i * chans, j, grads)
    back_all = grads[...].astype(BF16)
    back_in = back_all[: 3 * chans]
    back_out = back_all[3 * chans :]

    dx_part = dot(wj_ref[...], back_in)
    dx_out[...] = dx_part.reshape(groups, chans, span).astype(BF16)
    dx_copies = []
    for k in range(1, groups):
        to = lax.rem(mine + k, groups)
        dx_copies.append(
            remote(dx_out.at[to], dx_in.at[mine], sems_dx.at[0, k], sems_dx.at[1, k], (me, to))
        )
    share = width // seqs
    w_out_buf[:, :, : 3 * chans] = (dot_rows(x_all, back_in) * scale).reshape(
        seqs, share, 3 * chans
    )
    w_out_buf[:, :, 3 * chans :] = (dot_rows(g_all, back_out) * scale).reshape(seqs, share, chans)
    w_copies = exchange(w_out_buf, w_in_buf, 6)
    dx_in[mine] = dx_out[mine]

    finish(fg_copies)
    for j in range(seqs):
        unfold(fg_in[j, 0], 0, j, df1_ref)
        unfold(fg_in[j, 1], 0, j, df2_ref)
    finish(tap_copies)
    finish(dx_copies)
    total = dx_in[0].astype(F32)
    for j in range(1, groups):
        total = total + dx_in[j].astype(F32)
    dx_ref[...] = total.astype(BF16)
    finish(w_copies)
    total = w_in_buf[0]
    for j in range(1, seqs):
        total = total + w_in_buf[j]
    dw_ref[...] = total


def local(inputs, cotangent, w_in, short_taps, filter_one, filter_two, w_out):
    chans, span = inputs.shape
    seqs = lax.axis_size("seq")
    groups = lax.axis_size("ch")
    width = chans * groups
    own = chans // seqs
    piece = span // LANES * own
    share = width // seqs
    me = lax.axis_index("seq")
    w_turned = w_in.transpose(0, 2, 1).reshape(3 * chans, width)
    w_joined = w_in.transpose(1, 0, 2).reshape(width, 3 * chans)
    taps = lax.dynamic_slice_in_dim(short_taps.reshape(9, chans), me * own, own, axis=1)
    taps = jnp.broadcast_to(jnp.tile(taps, (1, 8 // own))[:, :, None], (9, 8, LANES))
    tables = [jnp.asarray(table) for table in dft_tables(span * seqs, own)]
    vmem = pl.BlockSpec(memory_space=pltpu.VMEM)
    dx, dw, dt, df1, df2 = pl.pallas_call(
        functools.partial(kernel, seqs, groups),
        out_shape=(
            jax.ShapeDtypeStruct((chans, span), BF16),
            jax.ShapeDtypeStruct((share, 4 * chans), F32),
            jax.ShapeDtypeStruct((seqs, 8, LANES), F32),
            jax.ShapeDtypeStruct((chans, span), F32),
            jax.ShapeDtypeStruct((chans, span), F32),
        ),
        in_specs=[vmem] * (8 + len(tables)),
        out_specs=(vmem,) * 5,
        scratch_shapes=[
            pltpu.VMEM((2, groups, chans, span), BF16),
            pltpu.VMEM((seqs, 2, piece, LANES), F32),
            pltpu.VMEM((seqs, 2, piece, LANES), F32),
            pltpu.VMEM((seqs, 4, piece, LANES), F32),
            pltpu.VMEM((seqs, 4, piece, LANES), F32),
            pltpu.VMEM((seqs, piece, LANES), BF16),
            pltpu.VMEM((seqs, piece, LANES), BF16),
            pltpu.VMEM((seqs, 2, piece, LANES), F32),
            pltpu.VMEM((seqs, 2, piece, LANES), F32),
            pltpu.VMEM((seqs, 3, piece, LANES), BF16),
            pltpu.VMEM((seqs, 3, piece, LANES), BF16),
            pltpu.VMEM((4 * chans, span), F32),
            pltpu.VMEM((seqs, share, 4 * chans), F32),
            pltpu.VMEM((seqs, share, 4 * chans), F32),
            pltpu.VMEM((groups, chans, span), BF16),
            pltpu.VMEM((groups, chans, span), BF16),
            pltpu.SemaphoreType.DMA((2, 2, groups)),
            pltpu.SemaphoreType.DMA((2, 7, seqs)),
            pltpu.SemaphoreType.DMA((2, groups)),
        ],
        compiler_params=pltpu.CompilerParams(
            collective_id=0, has_side_effects=True, vmem_limit_bytes=40 * 1024 * 1024
        ),
    )(inputs, cotangent, filter_one, filter_two, w_turned, w_joined, w_out, taps, *tables)
    w_in_grad = dw[:, : 3 * chans].reshape(share, 3, chans).transpose(1, 0, 2)
    w_out_grad = dw[:, 3 * chans :].T
    taps_grad = dt[:, :, :9].reshape(seqs, 8 // own, own, 9).sum(axis=1)
    taps_grad = taps_grad.reshape(chans, 9).T.reshape(3, 3, chans)
    return (dx, w_in_grad, taps_grad, df1, df2, w_out_grad)


def solution(mesh):
    in_specs = (
        P("ch", "seq"),
        P("ch", "seq"),
        P(None, None, "ch"),
        P(None, None, "ch"),
        P("ch", "seq"),
        P("ch", "seq"),
        P("ch", None),
    )
    out_specs = (
        P("ch", "seq"),
        P(None, "seq", "ch"),
        P(None, None, "ch"),
        P("ch", "seq"),
        P("ch", "seq"),
        P("ch", "seq"),
    )
    return jax.shard_map(local, mesh=mesh, in_specs=in_specs, out_specs=out_specs, check_vma=False)
```

time: 549 us -> 65.4 us (0.12); the launches traced: 542 us -> 64.6 us
  waiting for transfers between devices: 225 us -> 0 us
  blocking collectives: 138 us -> 0 us
  matrix products: 62.2 us -> 0 us
  Pallas kernels: 0 us -> 46.2 us
  starting transfers between devices: 39.6 us -> 0 us
  other arithmetic: 28.8 us -> 0 us
  local copies, waits for them, and re-layouts: 33 us -> 17.7 us
  between operations: 16 us -> 0.72 us
    reduce_scatter x2 -> x0, waiting for transfers between devices: 125 us -> none  [the longest x1 65.4 us: local(): lax.psum_scatter(in_terms, 'seq', scatter_dimension=1, tiled=True)]
    all_to_all x7 -> x0, blocking collectives: 105 us -> none  [the longest x2 46 us: inverse_transform(): lax.all_to_all(blocks, 'seq', split_axis=2, concat_axis=3, tiled=True)]
    all_to_all x9 -> x0, waiting for transfers between devices: 94.9 us -> none  [the longest x3 45.6 us: forward_transform(): lax.all_to_all(blocks, 'seq', split_axis=3, concat_axis=2, tiled=True)]
    dot_general x85 -> x0, matrix products: 62.2 us -> none  [the longest x16 13.4 us: rotate(): jnp.einsum(pattern, table_sin, imag_part, precision=lax.Precision.HIGHEST)]
    pallas_call x0 -> x1, Pallas kernels: none -> 46.2 us  [local(): pl.pallas_call(functools.partial(kernel, seqs, groups), out_shape=(jax.Sh...]
    all_to_all x9 -> x0, starting transfers between devices: 34.7 us -> none  [the longest x3 11.9 us: forward_transform(): lax.all_to_all(blocks, 'seq', split_axis=3, concat_axis=2, tiled=True)]
    psum x1 -> x0, blocking collectives: 19.6 us -> none  [local(): lax.psum(tap_terms, 'seq').reshape(3, 3, chans).transpose(1, 0, 2)]
    all_gather x2 -> x0, blocking collectives: 13.5 us -> none  [the longest x1 7.54 us: local(): lax.all_gather(inputs, 'ch', axis=0, tiled=True)]
  transfers between devices with their start and end apart: 14 -> 0, of which waited for: 12 -> 0; matrix products, arithmetic and copies ran while one was open for 9% -> 0% of each run, Pallas kernels for 0% -> 0%
where the time goes in v1:
time: 65.4 us; the launch traced here: 64.6 us
  Pallas kernels  46.2 us (71%)
  local copies, waits for them, and re-layouts  17.7 us (27%)
  between operations  0.72 us (1%)
    pallas_call x1, Pallas kernels, local(): pl.pallas_call(functools.partial(kernel, seqs, groups), out_shape=(jax.Sh...  46.2 us
    unnamed x38, local copies, waits for them, and re-layouts  15 us

profile of v1, /device:TPU:0, one launch (start us, length us, event | category | flops | bytes accessed | tf_op | source)
XLA Modules:
  0.0 64.6 jit_solution(8902919983808566427)
XLA Ops:
  0.6 0.7 %copy-done.16 = f32[3,3,64]{2,1,0:T(4,128)S(1)} copy-done((f32[3,3,64]{2,1,0:T(4,128)S(1)}, f32[3,3,64]{2,1,0:T(4,128)}, u32[]{:S(2)}) %copy-start.16) | copy-done | bytes 2328
  1.3 0.1 constant_dynamic-slice_fusion
  1.5 1.1 %copy.26.wj_ref = bf16[256,192]{1,0:T(8,128)(2,1)S(1)} copy(bf16[256,192]{0,1:T(8,128)(2,1)} %bitcast.14) | data formatting | bytes 196608 | tf_op jit(solution)/shard_map/reshape | solution.py:381
  2.6 0.9 %copy-done.1 = bf16[256,512]{1,0:T(8,128)(2,1)S(1)} copy-done((bf16[256,512]{1,0:T(8,128)(2,1)S(1)}, bf16[256,512]{1,0:T(8,128)(2,1)}, u32[]{:S(2)}) %copy-start.1) | copy-done | bytes 262168
  3.6 0.9 %copy-done.2 = bf16[256,512]{1,0:T(8,128)(2,1)S(1)} copy-done((bf16[256,512]{1,0:T(8,128)(2,1)S(1)}, bf16[256,512]{1,0:T(8,128)(2,1)}, u32[]{:S(2)}) %copy-start.2) | copy-done | bytes 262168
  4.5 0.9 %copy-done.3 = bf16[512,256]{1,0:T(8,128)(2,1)S(1)} copy-done((bf16[512,256]{1,0:T(8,128)(2,1)S(1)}, bf16[512,256]{1,0:T(8,128)(2,1)}, u32[]{:S(2)}) %copy-start.3) | copy-done | bytes 262168
  5.5 0.9 %copy-done.4 = bf16[512,256]{1,0:T(8,128)(2,1)S(1)} copy-done((bf16[512,256]{1,0:T(8,128)(2,1)S(1)}, bf16[512,256]{1,0:T(8,128)(2,1)}, u32[]{:S(2)}) %copy-start.4) | copy-done | bytes 262168
  6.4 0.9 %copy-done.6 = f32[64,512]{1,0:T(8,128)S(1)} copy-done((f32[64,512]{1,0:T(8,128)S(1)}, f32[64,512]{1,0:T(8,128)}, u32[]{:S(2)}) %copy-start.6) | copy-done | bytes 131096
  7.3 0.9 %copy-done.7 = f32[256,128]{1,0:T(8,128)S(1)} copy-done((f32[256,128]{1,0:T(8,128)S(1)}, f32[256,128]{1,0:T(8,128)}, u32[]{:S(2)}) %copy-start.7) | copy-done | bytes 131096
  8.2 0.9 %copy-done.8 = f32[256,128]{1,0:T(8,128)S(1)} copy-done((f32[256,128]{1,0:T(8,128)S(1)}, f32[256,128]{1,0:T(8,128)}, u32[]{:S(2)}) %copy-start.8) | copy-done | bytes 131096
  9.1 0.9 %copy-done.9 = bf16[256,256]{1,0:T(8,128)(2,1)S(1)} copy-done((bf16[256,256]{1,0:T(8,128)(2,1)S(1)}, bf16[256,256]{1,0:T(8,128)(2,1)}, u32[]{:S(2)}) %copy-start.9) | copy-done | bytes 131096
  10.0 0.9 %copy-done.10 = bf16[256,256]{1,0:T(8,128)(2,1)S(1)} copy-done((bf16[256,256]{1,0:T(8,128)(2,1)S(1)}, bf16[256,256]{1,0:T(8,128)(2,1)}, u32[]{:S(2)}) %copy-start.10) | copy-done | bytes 131096
  10.9 0.9 %copy-done.11 = bf16[256,256]{1,0:T(8,128)(2,1)S(1)} copy-done((bf16[256,256]{1,0:T(8,128)(2,1)S(1)}, bf16[256,256]{1,0:T(8,128)(2,1)}, u32[]{:S(2)}) %copy-start.11) | copy-done | bytes 131096
  11.8 0.9 %copy-done.12 = bf16[256,256]{1,0:T(8,128)(2,1)S(1)} copy-done((bf16[256,256]{1,0:T(8,128)(2,1)S(1)}, bf16[256,256]{1,0:T(8,128)(2,1)}, u32[]{:S(2)}) %copy-start.12) | copy-done | bytes 131096
  12.7 0.8 %copy-done.14 = bf16[64,512]{1,0:T(8,128)(2,1)S(1)} copy-done((bf16[64,512]{1,0:T(8,128)(2,1)S(1)}, bf16[64,512]{1,0:T(8,128)(2,1)}, u32[]{:S(2)}) %copy-start.14) | copy-done | bytes 65560
  13.6 0.8 %copy-done.15 = bf16[64,256]{1,0:T(8,128)(2,1)S(1)} copy-done((bf16[64,256]{1,0:T(8,128)(2,1)S(1)}, bf16[64,256]{1,0:T(8,128)(2,1)}, u32[]{:S(2)}) %copy-start.15) | copy-done | bytes 32792
  14.3 46.2 %shard_map.208 = (bf16[64,512]{1,0:T(8,128)(2,1)S(1)}, f32[32,256]{1,0:T(8,128)S(1)}, f32[8,8,128]{2,1,0:T(8,128)S(1)}, f32[64,512]{1,0:T(8,128)S(1)}, f32[64,512]{1,0:T(8,128)S(1)}) custom-call(bf16[64,512]{1,0:T(8,128)(2,1)S(1)} %copy-done.13, bf16[64,512]{1,0:T(8,128)(2,1)S(1)} %copy-done.14, f32[64,512]{1,0:T(8,128)S(1)} %copy-done.5, ...), custom_call_target="tpu_custom_call" | custom-call | tf_op jit(solution)/shard_map/pallas_call | solution.py:386
  60.6 0.7 %slice_bitcast_fusion.1 = f32[64,32]{0,1:T(8,128)} fusion(f32[32,256]{1,0:T(8,128)S(1)} %get-tuple-element.12), kind=kLoop, calls=%fused_computation.1 | loop fusion | bytes 16384 | tf_op jit(solution)/shard_map/transpose | solution.py:423
  61.3 0.6 reshape.40
  61.9 0.1 reshape.38
  62.0 0.6 copy.28
  62.6 0.6 copy.32
  63.3 0.7 %copy.33 = f32[64,512]{1,0:T(8,128)} copy(f32[64,512]{1,0:T(8,128)S(1)} %get-tuple-element.31) | data formatting | bytes 262144
  63.9 0.7 %copy.34 = f32[64,512]{1,0:T(8,128)} copy(f32[64,512]{1,0:T(8,128)S(1)} %get-tuple-element.32) | data formatting | bytes 262144
  (24 shorter events, 0.2 us)
Async XLA Ops:
  0.6 0.7 %copy-start.16 = (f32[3,3,64]{2,1,0:T(4,128)S(1)}, f32[3,3,64]{2,1,0:T(4,128)}, u32[]{:S(2)}) copy-start(f32[3,3,64]{2,1,0:T(4,128)} %param.20) | copy-start | bytes 6916
  1.3 1.2 %copy-start.13 = (bf16[64,512]{1,0:T(8,128)(2,1)S(1)}, bf16[64,512]{1,0:T(8,128)(2,1)}, u32[]{:S(2)}) copy-start(bf16[64,512]{1,0:T(8,128)(2,1)} %x_ref.1) | copy-start | bytes 196612
  1.4 1.2 %copy-start.5 = (f32[64,512]{1,0:T(8,128)S(1)}, f32[64,512]{1,0:T(8,128)}, u32[]{:S(2)}) copy-start(f32[64,512]{1,0:T(8,128)} %f1_ref.1) | copy-start | bytes 393220
  1.5 1.1 %copy-start = (bf16[3,256,64]{1,2,0:T(8,128)(2,1)S(1)}, bf16[3,256,64]{1,2,0:T(8,128)(2,1)}, u32[]{:S(2)}) copy-start(bf16[3,256,64]{1,2,0:T(8,128)(2,1)} %param.19) | copy-start | bytes 294916
  2.6 1.0 %copy-start.1 = (bf16[256,512]{1,0:T(8,128)(2,1)S(1)}, bf16[256,512]{1,0:T(8,128)(2,1)}, u32[]{:S(2)}) copy-start(bf16[256,512]{1,0:T(8,128)(2,1)} %constant.36.clone.mi_lo) | copy-start | bytes 786436
  3.6 0.9 %copy-start.2 = (bf16[256,512]{1,0:T(8,128)(2,1)S(1)}, bf16[256,512]{1,0:T(8,128)(2,1)}, u32[]{:S(2)}) copy-start(bf16[256,512]{1,0:T(8,128)(2,1)} %constant.35.clone.mi_hi) | copy-start | bytes 786436
  4.5 0.9 %copy-start.3 = (bf16[512,256]{1,0:T(8,128)(2,1)S(1)}, bf16[512,256]{1,0:T(8,128)(2,1)}, u32[]{:S(2)}) copy-start(bf16[512,256]{1,0:T(8,128)(2,1)} %constant.34.clone.mf_lo) | copy-start | bytes 786436
  5.5 0.9 %copy-start.4 = (bf16[512,256]{1,0:T(8,128)(2,1)S(1)}, bf16[512,256]{1,0:T(8,128)(2,1)}, u32[]{:S(2)}) copy-start(bf16[512,256]{1,0:T(8,128)(2,1)} %constant.33.clone.mf_hi) | copy-start | bytes 786436
  6.4 0.9 %copy-start.6 = (f32[64,512]{1,0:T(8,128)S(1)}, f32[64,512]{1,0:T(8,128)}, u32[]{:S(2)}) copy-start(f32[64,512]{1,0:T(8,128)} %f2_ref.1) | copy-start | bytes 393220
  7.3 0.9 %copy-start.7 = (f32[256,128]{1,0:T(8,128)S(1)}, f32[256,128]{1,0:T(8,128)}, u32[]{:S(2)}) copy-start(f32[256,128]{1,0:T(8,128)} %constant.42.clone.ts_ref) | copy-start | bytes 393220
  8.2 0.9 %copy-start.8 = (f32[256,128]{1,0:T(8,128)S(1)}, f32[256,128]{1,0:T(8,128)}, u32[]{:S(2)}) copy-start(f32[256,128]{1,0:T(8,128)} %constant.41.clone.tc_ref) | copy-start | bytes 393220
  9.1 0.9 %copy-start.9 = (bf16[256,256]{1,0:T(8,128)(2,1)S(1)}, bf16[256,256]{1,0:T(8,128)(2,1)}, u32[]{:S(2)}) copy-start(bf16[256,256]{1,0:T(8,128)(2,1)} %constant.40.clone.di_lo) | copy-start | bytes 393220
  10.0 0.9 %copy-start.10 = (bf16[256,256]{1,0:T(8,128)(2,1)S(1)}, bf16[256,256]{1,0:T(8,128)(2,1)}, u32[]{:S(2)}) copy-start(bf16[256,256]{1,0:T(8,128)(2,1)} %constant.39.clone.di_hi) | copy-start | bytes 393220
  10.9 0.9 %copy-start.11 = (bf16[256,256]{1,0:T(8,128)(2,1)S(1)}, bf16[256,256]{1,0:T(8,128)(2,1)}, u32[]{:S(2)}) copy-start(bf16[256,256]{1,0:T(8,128)(2,1)} %constant.38.clone.df_lo) | copy-start | bytes 393220
  11.8 0.9 %copy-start.12 = (bf16[256,256]{1,0:T(8,128)(2,1)S(1)}, bf16[256,256]{1,0:T(8,128)(2,1)}, u32[]{:S(2)}) copy-start(bf16[256,256]{1,0:T(8,128)(2,1)} %constant.37.clone.df_hi) | copy-start | bytes 393220
  12.7 0.8 %copy-start.14 = (bf16[64,512]{1,0:T(8,128)(2,1)S(1)}, bf16[64,512]{1,0:T(8,128)(2,1)}, u32[]{:S(2)}) copy-start(bf16[64,512]{1,0:T(8,128)(2,1)} %g_ref.1) | copy-start | bytes 196612
  13.6 0.8 %copy-start.15 = (bf16[64,256]{1,0:T(8,128)(2,1)S(1)}, bf16[64,256]{1,0:T(8,128)(2,1)}, u32[]{:S(2)}) copy-start(bf16[64,256]{1,0:T(8,128)(2,1)} %wo_ref.1) | copy-start | bytes 98308

commit v2 on v1

--- a/solution.py
+++ b/solution.py
@@ -11,6 +11,7 @@
 from jax.sharding import PartitionSpec as P
 
 LANES = 128
+TABLES = 10
 MESH = pl.DeviceIdType.MESH
 BF16 = jnp.bfloat16
 F32 = jnp.float32
@@ -57,6 +58,11 @@
     return lax.dot_general(left, right, (((1,), (1,)), ((), ())), preferred_element_type=F32)
 
 
+def spread(value, first, own, target):
+    for q in range(target.shape[1] // LANES):
+        target[first : first + own, q * LANES : (q + 1) * LANES] = value[q * own : (q + 1) * own]
+
+
 def kernel(
     seqs,
     groups,
@@ -64,45 +70,38 @@
     g_ref,
     f1_ref,
     f2_ref,
-    wt_ref,
-    wj_ref,
+    w_ref,
     wo_ref,
     taps_ref,
-    mf_hi,
-    mf_lo,
-    mi_hi,
-    mi_lo,
-    df_hi,
-    df_lo,
-    di_hi,
-    di_lo,
-    tc_ref,
-    ts_ref,
-    dx_ref,
-    dw_ref,
-    dt_ref,
-    df1_ref,
-    df2_ref,
-    xg,
-    filt_out,
-    filt_in,
-    sig_out,
-    sig_in,
-    gated_out,
-    gated_in,
-    fg_out,
-    fg_in,
-    pg_out,
-    pg_in,
-    grads,
-    w_out_buf,
-    w_in_buf,
-    dx_out,
-    dx_in,
-    sems_x,
-    sems_seq,
-    sems_dx,
+    *rest,
 ):
+    sources, rest = rest[:TABLES], rest[TABLES:]
+    w_in_buf, dt_ref, fg_in, dx_in = rest[:4]
+    tables, rest = rest[4 : 4 + TABLES], rest[4 + TABLES :]
+    mf_hi, mf_lo, mi_hi, mi_lo, df_hi, df_lo, di_hi, di_lo, tc_ref, ts_ref = tables
+    (
+        filters,
+        w_here,
+        wo_here,
+        xg,
+        filt_out,
+        filt_in,
+        sig_fold,
+        sig_out,
+        sig_in,
+        gated_out,
+        gated_in,
+        fg_out,
+        pg_out,
+        pg_in,
+        grads,
+        w_out_buf,
+        dx_out,
+        sems_x,
+        sems_seq,
+        sems_dx,
+        sems_local,
+    ) = rest
     chans, span = x_ref.shape
     own = chans // seqs
     parts = span // LANES
@@ -123,15 +122,25 @@
             barrier, inc=1, device_id=(me, lax.rem(mine + k, groups)), device_id_type=MESH
         )
 
+    arrivals = [
+        (f1_ref, filters.at[0]),
+        (f2_ref, filters.at[1]),
+        (w_ref, w_here),
+        (wo_ref, wo_here),
+        (x_ref, xg.at[0, mine]),
+        (g_ref, xg.at[1, mine]),
+    ] + list(zip(sources, tables))
+    fetches = []
+    for at, (source, target) in enumerate(arrivals):
+        fetch = pltpu.make_async_copy(source, target, sems_local.at[at])
+        fetch.start()
+        fetches.append(fetch)
+
     def fold(value, first, target, index):
         for q in range(parts):
             target[index + (pl.ds(q * own, own), slice(None))] = value[
                 first : first + own, q * LANES : (q + 1) * LANES
             ]
-
-    for j in range(seqs):
-        fold(f1_ref[pl.ds(j * own, own), :], 0, filt_out, (j, 0))
-        fold(f2_ref[pl.ds(j * own, own), :], 0, filt_out, (j, 1))
 
     pl.semaphore_wait(barrier, seqs - 1 + groups - 1)
 
@@ -171,18 +180,24 @@
         for copy in copies:
             copy.wait()
 
+    fetches[0].wait()
+    fetches[1].wait()
+    for j in range(seqs):
+        for i in range(2):
+            fold(filters[i, pl.ds(j * own, own), :], 0, filt_out, (j, i))
     filt_copies = exchange(filt_out, filt_in, 0)
-    xg[0, mine] = x_ref[...]
-    xg[1, mine] = g_ref[...]
+    finish(fetches[2:])
+    w_turned = w_here[...].reshape(3 * chans, width)
     finish(x_copies)
     x_all = xg[0].reshape(width, span)
     g_all = xg[1].reshape(width, span)
-    projected = dot(wt_ref[...], x_all)
-    gated_grad_here = dot(wo_ref[...], g_all)
+    projected = dot(w_turned, x_all)
+    gated_grad_here = dot(wo_here[...], g_all)
     for j in range(seqs):
         for i in range(3):
-            fold(projected, i * chans + j * own, sig_out, (j, i))
-        fold(gated_grad_here, j * own, sig_out, (j, 3))
+            fold(projected, i * chans + j * own, sig_fold, (j, i))
+        fold(gated_grad_here, j * own, sig_fold, (j, 3))
+    sig_out[...] = sig_fold[...].astype(BF16)
     sig_copies = exchange(sig_out, sig_in, 1)
 
     cos_twist = tc_ref[...]
@@ -238,9 +253,12 @@
     def conj_times(a, b):
         return (a[0] * b[0] + a[1] * b[1], a[0] * b[1] - a[1] * b[0])
 
+    def gathered(block):
+        return block.astype(F32).reshape(rows, LANES)
+
     finish(filt_copies)
     spec_one, spec_two = forward(
-        [filt_in[:, 0].reshape(rows, LANES), filt_in[:, 1].reshape(rows, LANES)]
+        [gathered(filt_in[:, 0]), gathered(filt_in[:, 1])]
     )
 
     row = lax.broadcasted_iota(jnp.int32, (rows, LANES), 0)
@@ -263,7 +281,7 @@
     finish(sig_copies)
 
     def projection(i):
-        value = sig_in[:, i].reshape(rows, LANES)
+        value = gathered(sig_in[:, i])
         return value, delayed(value, 1), delayed(value, 2)
 
     def filtered(i):
@@ -273,7 +291,7 @@
     gate_one = filtered(0)
     gate_two = filtered(1)
     value = filtered(2)
-    gated_grad = sig_in[:, 3].reshape(rows, LANES)
+    gated_grad = gathered(sig_in[:, 3])
 
     second_grad = gated_grad * gate_two
     spec_value, spec_second = forward([value, second_grad])
@@ -288,6 +306,8 @@
     gated = gate_two * second
     gated_out[...] = gated.reshape(seqs, piece, LANES).astype(BF16)
     gated_copies = exchange(gated_out, gated_in, 2)
+    fg_out[1] = (filter_two_grad * scale).reshape(seqs, piece, LANES).astype(BF16)
+    fg_copies = exchange(fg_out.at[1], fg_in.at[1], 4)
     value_grad, filter_one_grad = inverse(
         [conj_times(spec_one, spec_first), conj_times(spec_value, spec_first)]
     )
@@ -297,9 +317,8 @@
         back = tap(i, 0) * grad + tap(i, 1) * advanced(grad, 1) + tap(i, 2) * advanced(grad, 2)
         pg_out[:, i] = back.reshape(seqs, piece, LANES).astype(BF16)
     pg_copies = exchange(pg_out, pg_in, 3)
-    fg_out[:, 0] = (filter_one_grad * scale).reshape(seqs, piece, LANES)
-    fg_out[:, 1] = (filter_two_grad * scale).reshape(seqs, piece, LANES)
-    fg_copies = exchange(fg_out, fg_in, 4)
+    fg_out[0] = (filter_one_grad * scale).reshape(seqs, piece, LANES).astype(BF16)
+    fg_copies += exchange(fg_out.at[0], fg_in.at[0], 7)
 
     small_lane = lax.broadcasted_iota(jnp.int32, (8, LANES), 1)
     tap_terms = jnp.zeros((8, LANES), F32)
@@ -319,10 +338,7 @@
         )
 
     def unfold(value, first, source, target):
-        for q in range(parts):
-            target[pl.ds(first + source * own, own), q * LANES : (q + 1) * LANES] = value[
-                q * own : (q + 1) * own, :
-            ]
+        spread(value, first + source * own, own, target)
 
     finish(gated_copies)
     for j in range(seqs):
@@ -335,8 +351,10 @@
     back_in = back_all[: 3 * chans]
     back_out = back_all[3 * chans :]
 
-    dx_part = dot(wj_ref[...], back_in)
-    dx_out[...] = dx_part.reshape(groups, chans, span).astype(BF16)
+    dx_part = lax.dot_general(
+        w_turned, back_in, (((0,), (0,)), ((), ())), preferred_element_type=F32
+    )
+    dx_out[...] = dx_part.reshape(groups, chans, span)
     dx_copies = []
     for k in range(1, groups):
         to = lax.rem(mine + k, groups)
@@ -346,26 +364,43 @@
     share = width // seqs
     w_out_buf[:, :, : 3 * chans] = (dot_rows(x_all, back_in) * scale).reshape(
         seqs, share, 3 * chans
-    )
-    w_out_buf[:, :, 3 * chans :] = (dot_rows(g_all, back_out) * scale).reshape(seqs, share, chans)
+    ).astype(BF16)
+    w_out_buf[:, :, 3 * chans :] = (dot_rows(g_all, back_out) * scale).reshape(seqs, share, chans).astype(BF16)
     w_copies = exchange(w_out_buf, w_in_buf, 6)
     dx_in[mine] = dx_out[mine]
 
     finish(fg_copies)
-    for j in range(seqs):
-        unfold(fg_in[j, 0], 0, j, df1_ref)
-        unfold(fg_in[j, 1], 0, j, df2_ref)
     finish(tap_copies)
     finish(dx_copies)
-    total = dx_in[0].astype(F32)
-    for j in range(1, groups):
-        total = total + dx_in[j].astype(F32)
+    finish(w_copies)
+
+
+def closing(w_ref, dt_ref, fg_ref, dx_part_ref, dx_ref, dw_in_ref, taps_ref, df1_ref, df2_ref, dw_out_ref):
+    seqs = w_ref.shape[0]
+    chans = dx_ref.shape[0]
+    own = chans // seqs
+    for j in range(seqs):
+        for ref, i in ((df1_ref, 0), (df2_ref, 1)):
+            spread(fg_ref[i, j].astype(F32), j * own, own, ref)
+    total = dx_part_ref[0].astype(F32)
+    for j in range(1, dx_part_ref.shape[0]):
+        total = total + dx_part_ref[j].astype(F32)
     dx_ref[...] = total.astype(BF16)
-    finish(w_copies)
-    total = w_in_buf[0]
+    total = w_ref[0].astype(F32)
     for j in range(1, seqs):
-        total = total + w_in_buf[j]
-    dw_ref[...] = total
+        total = total + w_ref[j].astype(F32)
+    for i in range(3):
+        dw_in_ref[i] = total[:, i * chans : (i + 1) * chans]
+    dw_out_ref[...] = total[:, 3 * chans :]
+    terms = []
+    for j in range(seqs):
+        term = dt_ref[j, 0:own]
+        for r in range(own, 8, own):
+            term = term + dt_ref[j, r : r + own]
+        terms.append(term)
+    turned = jnp.concatenate(terms, axis=0).T
+    for i in range(3):
+        taps_ref[i] = turned[3 * i : 3 * i + 3, :]
 
 
 def local(inputs, cotangent, w_in, short_taps, filter_one, filter_two, w_out):
@@ -377,53 +412,67 @@
     piece = span // LANES * own
     share = width // seqs
     me = lax.axis_index("seq")
-    w_turned = w_in.transpose(0, 2, 1).reshape(3 * chans, width)
-    w_joined = w_in.transpose(1, 0, 2).reshape(width, 3 * chans)
+    w_turned = w_in.transpose(0, 2, 1)
     taps = lax.dynamic_slice_in_dim(short_taps.reshape(9, chans), me * own, own, axis=1)
     taps = jnp.broadcast_to(jnp.tile(taps, (1, 8 // own))[:, :, None], (9, 8, LANES))
     tables = [jnp.asarray(table) for table in dft_tables(span * seqs, own)]
     vmem = pl.BlockSpec(memory_space=pltpu.VMEM)
-    dx, dw, dt, df1, df2 = pl.pallas_call(
+    hbm = pl.BlockSpec(memory_space=pltpu.HBM)
+    received = pl.pallas_call(
         functools.partial(kernel, seqs, groups),
         out_shape=(
-            jax.ShapeDtypeStruct((chans, span), BF16),
-            jax.ShapeDtypeStruct((share, 4 * chans), F32),
+            jax.ShapeDtypeStruct((seqs, share, 4 * chans), BF16),
             jax.ShapeDtypeStruct((seqs, 8, LANES), F32),
-            jax.ShapeDtypeStruct((chans, span), F32),
-            jax.ShapeDtypeStruct((chans, span), F32),
+            jax.ShapeDtypeStruct((2, seqs, piece, LANES), BF16),
+            jax.ShapeDtypeStruct((groups, chans, span), F32),
         ),
-        in_specs=[vmem] * (8 + len(tables)),
-        out_specs=(vmem,) * 5,
-        scratch_shapes=[
+        in_specs=[hbm] * 6 + [vmem] + [hbm] * TABLES,
+        out_specs=(vmem,) * 4,
+        scratch_shapes=[pltpu.VMEM(table.shape, table.dtype) for table in tables]
+        + [
+            pltpu.VMEM((2, chans, span), F32),
+            pltpu.VMEM(w_turned.shape, BF16),
+            pltpu.VMEM(w_out.shape, BF16),
             pltpu.VMEM((2, groups, chans, span), BF16),
             pltpu.VMEM((seqs, 2, piece, LANES), F32),
             pltpu.VMEM((seqs, 2, piece, LANES), F32),
             pltpu.VMEM((seqs, 4, piece, LANES), F32),
-            pltpu.VMEM((seqs, 4, piece, LANES), F32),
+            pltpu.VMEM((seqs, 4, piece, LANES), BF16),
+            pltpu.VMEM((seqs, 4, piece, LANES), BF16),
             pltpu.VMEM((seqs, piece, LANES), BF16),
             pltpu.VMEM((seqs, piece, LANES), BF16),
-            pltpu.VMEM((seqs, 2, piece, LANES), F32),
-            pltpu.VMEM((seqs, 2, piece, LANES), F32),
+            pltpu.VMEM((2, seqs, piece, LANES), BF16),
             pltpu.VMEM((seqs, 3, piece, LANES), BF16),
             pltpu.VMEM((seqs, 3, piece, LANES), BF16),
             pltpu.VMEM((4 * chans, span), F32),
-            pltpu.VMEM((seqs, share, 4 * chans), F32),
-            pltpu.VMEM((seqs, share, 4 * chans), F32),
-            pltpu.VMEM((groups, chans, span), BF16),
-            pltpu.VMEM((groups, chans, span), BF16),
+            pltpu.VMEM((seqs, share, 4 * chans), BF16),
+            pltpu.VMEM((groups, chans, span), F32),
             pltpu.SemaphoreType.DMA((2, 2, groups)),
-            pltpu.SemaphoreType.DMA((2, 7, seqs)),
+            pltpu.SemaphoreType.DMA((2, 8, seqs)),
             pltpu.SemaphoreType.DMA((2, groups)),
+            pltpu.SemaphoreType.DMA((6 + TABLES,)),
         ],
         compiler_params=pltpu.CompilerParams(
-            collective_id=0, has_side_effects=True, vmem_limit_bytes=40 * 1024 * 1024
+            collective_id=0, has_side_effects=True, vmem_limit_bytes=60 * 1024 * 1024
         ),
-    )(inputs, cotangent, filter_one, filter_two, w_turned, w_joined, w_out, taps, *tables)
-    w_in_grad = dw[:, : 3 * chans].reshape(share, 3, chans).transpose(1, 0, 2)
-    w_out_grad = dw[:, 3 * chans :].T
-    taps_grad = dt[:, :, :9].reshape(seqs, 8 // own, own, 9).sum(axis=1)
-    taps_grad = taps_grad.reshape(chans, 9).T.reshape(3, 3, chans)
-    return (dx, w_in_grad, taps_grad, df1, df2, w_out_grad)
+    )(inputs, cotangent, filter_one, filter_two, w_turned, w_out, taps, *tables)
+    dx, w_in_grad, taps_grad, df1, df2, w_out_turned = (
+        pl.pallas_call(
+            closing,
+            out_shape=(
+                jax.ShapeDtypeStruct((chans, span), BF16),
+                jax.ShapeDtypeStruct((3, share, chans), F32),
+                jax.ShapeDtypeStruct((3, 3, chans), F32),
+                jax.ShapeDtypeStruct((chans, span), F32),
+                jax.ShapeDtypeStruct((chans, span), F32),
+                jax.ShapeDtypeStruct((share, chans), F32),
+            ),
+            in_specs=[vmem] * 4,
+            out_specs=(vmem,) * 6,
+            compiler_params=pltpu.CompilerParams(vmem_limit_bytes=60 * 1024 * 1024),
+        )(*received)
+    )
+    return (dx, w_in_grad, taps_grad, df1, df2, w_out_turned.T)
 
 
 def solution(mesh):

time: 65.4 us -> 46.5 us (0.71)
  local copies, waits for them, and re-layouts: 17.7 us -> 1.46 us
  Pallas kernels: 46.2 us -> 44.1 us
    unnamed x38 -> x2, local copies, waits for them, and re-layouts: 15 us -> 0.68 us
    pallas_call x1, Pallas kernels: 46.2 us -> 42.2 us  [local(): pl.pallas_call(functools.partial(kernel, seqs, groups), out_shape=(jax.Sh...]
    pallas_call x0 -> x1, Pallas kernels: none -> 1.96 us  [local(): pl.pallas_call(closing, out_shape=(jax.ShapeDtypeStruct((chans, span), BF...]
    reshape x3 -> x0, local copies, waits for them, and re-layouts: 1.77 us -> none  [the longest x1 1.07 us: local(): w_joined = w_in.transpose(1, 0, 2).reshape(width, 3 * chans)]
    transpose x3 -> x0, local copies, waits for them, and re-layouts: 0.76 us -> none  [the longest x1 0.68 us: local(): w_out_grad = dw[:, 3 * chans:].T]
where the time goes in v2:
time: 46.5 us; the launch traced here: 46.2 us
  Pallas kernels  44.1 us (95%)
  local copies, waits for them, and re-layouts  1.46 us (3%)
  between operations  0.65 us (1%)
    pallas_call x1, Pallas kernels, local(): pl.pallas_call(functools.partial(kernel, seqs, groups), out_shape=(jax.Sh...  42.2 us
    pallas_call x1, Pallas kernels, local(): pl.pallas_call(closing, out_shape=(jax.ShapeDtypeStruct((chans, span), BF...  1.96 us

profile of v2, /device:TPU:0, one launch (start us, length us, event | category | flops | bytes accessed | tf_op | source)
XLA Modules:
  0.0 46.2 jit_solution(394130252700766461)
XLA Ops:
  0.6 0.0 copy-start
  0.6 0.7 %copy-done = f32[3,3,64]{2,1,0:T(4,128)S(1)} copy-done((f32[3,3,64]{2,1,0:T(4,128)S(1)}, f32[3,3,64]{2,1,0:T(4,128)}, u32[]{:S(2)}) %copy-start) | copy-done | bytes 2328
  1.3 0.1 constant_dynamic-slice_fusion
  1.4 0.7 %broadcast_in_dim.2.taps_ref = f32[9,8,128]{2,1,0:T(8,128)} broadcast(f32[9,8]{1,0:T(8,128)S(1)} %constant_dynamic-slice_fusion), dimensions={0,1} | broadcast | bytes 37152 | tf_op jit(solution)/shard_map/broadcast_in_dim | solution.py:417
  2.1 42.2 %shard_map.208 = (bf16[8,32,256]{2,1,0:T(8,128)(2,1)}, f32[8,8,128]{2,1,0:T(8,128)}, bf16[2,8,32,128]{3,2,1,0:T(8,128)(2,1)}, f32[4,64,512]{2,1,0:T(8,128)}) custom-call(bf16[64,512]{1,0:T(8,128)(2,1)} %x_ref.1, bf16[64,512]{1,0:T(8,128)(2,1)} %g_ref.1, f32[64,512]{1,0:T(8,128)} %f1_ref.1, f32[64,512]{1,0:T(8,128)} %f2_ref.1, bf16[3,64,256]{2,1,0:T(8,128)(2,1)} %bitcast.2, ...), custom_call_target="tpu_custom_call" | custom-call | tf_op jit(solution)/shard_map/pallas_call | solution.py:421
  44.3 2.0 %shard_map.209 = (bf16[64,512]{1,0:T(8,128)(2,1)}, f32[3,32,64]{2,1,0:T(8,128)}, f32[3,3,64]{2,1,0:T(4,128)}, f32[64,512]{1,0:T(8,128)}, f32[64,512]{1,0:T(8,128)}, /*index=5*/f32[32,64]{1,0:T(8,128)}) custom-call(bf16[8,32,256]{2,1,0:T(8,128)(2,1)} %get-tuple-element.16.w_ref, f32[8,8,128]{2,1,0:T(8,128)} %get-tuple-element.17.dt_ref, ...), custom_call_target="tpu_custom_call" | custom-call | tf_op jit(solution)/shard_map/pallas_call | solution.py:460
  (1 shorter events, 0.0 us)
Async XLA Ops:
  0.6 0.7 %copy-start = (f32[3,3,64]{2,1,0:T(4,128)S(1)}, f32[3,3,64]{2,1,0:T(4,128)}, u32[]{:S(2)}) copy-start(f32[3,3,64]{2,1,0:T(4,128)} %param.20) | copy-start | bytes 6916

commit v3 on v2

--- a/solution.py
+++ b/solution.py
@@ -89,6 +89,8 @@
         sig_fold,
         sig_out,
         sig_in,
+        gg_out,
+        gg_in,
         gated_out,
         gated_in,
         fg_out,
@@ -157,9 +159,9 @@
         return copy
 
     x_copies = []
-    for k in range(1, groups):
-        peer = (me, lax.rem(mine + k, groups))
-        for a, ref in enumerate((x_ref, g_ref)):
+    for a, ref in enumerate((x_ref, g_ref)):
+        for k in range(1, groups):
+            peer = (me, lax.rem(mine + k, groups))
             x_copies.append(
                 remote(ref, xg.at[a, mine], sems_x.at[0, a, k], sems_x.at[1, a, k], peer)
             )
@@ -188,17 +190,21 @@
     filt_copies = exchange(filt_out, filt_in, 0)
     finish(fetches[2:])
     w_turned = w_here[...].reshape(3 * chans, width)
-    finish(x_copies)
+    finish(x_copies[: groups - 1])
     x_all = xg[0].reshape(width, span)
-    g_all = xg[1].reshape(width, span)
     projected = dot(w_turned, x_all)
-    gated_grad_here = dot(wo_here[...], g_all)
     for j in range(seqs):
         for i in range(3):
             fold(projected, i * chans + j * own, sig_fold, (j, i))
+    sig_out[...] = sig_fold[:, :3].astype(BF16)
+    sig_copies = exchange(sig_out, sig_in, 1)
+    finish(x_copies[groups - 1 :])
+    g_all = xg[1].reshape(width, span)
+    gated_grad_here = dot(wo_here[...], g_all)
+    for j in range(seqs):
         fold(gated_grad_here, j * own, sig_fold, (j, 3))
-    sig_out[...] = sig_fold[...].astype(BF16)
-    sig_copies = exchange(sig_out, sig_in, 1)
+    gg_out[...] = sig_fold[:, 3].astype(BF16)
+    sig_copies += exchange(gg_out, gg_in, 8)
 
     cos_twist = tc_ref[...]
     sin_twist = ts_ref[...]
@@ -291,7 +297,7 @@
     gate_one = filtered(0)
     gate_two = filtered(1)
     value = filtered(2)
-    gated_grad = gathered(sig_in[:, 3])
+    gated_grad = gathered(gg_in[...])
 
     second_grad = gated_grad * gate_two
     spec_value, spec_second = forward([value, second_grad])
@@ -437,8 +443,10 @@
             pltpu.VMEM((seqs, 2, piece, LANES), F32),
             pltpu.VMEM((seqs, 2, piece, LANES), F32),
             pltpu.VMEM((seqs, 4, piece, LANES), F32),
-            pltpu.VMEM((seqs, 4, piece, LANES), BF16),
-            pltpu.VMEM((seqs, 4, piece, LANES), BF16),
+            pltpu.VMEM((seqs, 3, piece, LANES), BF16),
+            pltpu.VMEM((seqs, 3, piece, LANES), BF16),
+            pltpu.VMEM((seqs, piece, LANES), BF16),
+            pltpu.VMEM((seqs, piece, LANES), BF16),
             pltpu.VMEM((seqs, piece, LANES), BF16),
             pltpu.VMEM((seqs, piece, LANES), BF16),
             pltpu.VMEM((2, seqs, piece, LANES), BF16),
@@ -448,7 +456,7 @@
             pltpu.VMEM((seqs, share, 4 * chans), BF16),
             pltpu.VMEM((groups, chans, span), F32),
             pltpu.SemaphoreType.DMA((2, 2, groups)),
-            pltpu.SemaphoreType.DMA((2, 8, seqs)),
+            pltpu.SemaphoreType.DMA((2, 9, seqs)),
             pltpu.SemaphoreType.DMA((2, groups)),
             pltpu.SemaphoreType.DMA((6 + TABLES,)),
         ],

time: 46.5 us -> 46.1 us (level)
  no operation moved by 1% of the time
where the time goes in v3:
time: 46.1 us; the launch traced here: 45.9 us
  Pallas kernels  43.8 us (95%)
  local copies, waits for them, and re-layouts  1.46 us (3%)
  between operations  0.65 us (1%)
    pallas_call x1, Pallas kernels, local(): pl.pallas_call(functools.partial(kernel, seqs, groups), out_shape=(jax.Sh...  41.8 us
    pallas_call x1, Pallas kernels, local(): pl.pallas_call(closing, out_shape=(jax.ShapeDtypeStruct((chans, span), BF...  1.96 us

profile of v3, /device:TPU:0, one launch (start us, length us, event | category | flops | bytes accessed | tf_op | source)
XLA Modules:
  0.0 45.9 jit_solution(14692772729600648355)
XLA Ops:
  0.6 0.0 copy-start
  0.6 0.7 %copy-done = f32[3,3,64]{2,1,0:T(4,128)S(1)} copy-done((f32[3,3,64]{2,1,0:T(4,128)S(1)}, f32[3,3,64]{2,1,0:T(4,128)}, u32[]{:S(2)}) %copy-start) | copy-done | bytes 2328
  1.3 0.1 constant_dynamic-slice_fusion
  1.4 0.7 %broadcast_in_dim.2.taps_ref = f32[9,8,128]{2,1,0:T(8,128)} broadcast(f32[9,8]{1,0:T(8,128)S(1)} %constant_dynamic-slice_fusion), dimensions={0,1} | broadcast | bytes 37152 | tf_op jit(solution)/shard_map/broadcast_in_dim | solution.py:423
  2.1 41.8 %shard_map.208 = (bf16[8,32,256]{2,1,0:T(8,128)(2,1)}, f32[8,8,128]{2,1,0:T(8,128)}, bf16[2,8,32,128]{3,2,1,0:T(8,128)(2,1)}, f32[4,64,512]{2,1,0:T(8,128)}) custom-call(bf16[64,512]{1,0:T(8,128)(2,1)} %x_ref.1, bf16[64,512]{1,0:T(8,128)(2,1)} %g_ref.1, f32[64,512]{1,0:T(8,128)} %f1_ref.1, f32[64,512]{1,0:T(8,128)} %f2_ref.1, bf16[3,64,256]{2,1,0:T(8,128)(2,1)} %bitcast.2, ...), custom_call_target="tpu_custom_call" | custom-call | tf_op jit(solution)/shard_map/pallas_call | solution.py:427
  43.9 2.0 %shard_map.209 = (bf16[64,512]{1,0:T(8,128)(2,1)}, f32[3,32,64]{2,1,0:T(8,128)}, f32[3,3,64]{2,1,0:T(4,128)}, f32[64,512]{1,0:T(8,128)}, f32[64,512]{1,0:T(8,128)}, /*index=5*/f32[32,64]{1,0:T(8,128)}) custom-call(bf16[8,32,256]{2,1,0:T(8,128)(2,1)} %get-tuple-element.16.w_ref, f32[8,8,128]{2,1,0:T(8,128)} %get-tuple-element.17.dt_ref, ...), custom_call_target="tpu_custom_call" | custom-call | tf_op jit(solution)/shard_map/pallas_call | solution.py:468
  (1 shorter events, 0.0 us)
Async XLA Ops:
  0.6 0.7 %copy-start = (f32[3,3,64]{2,1,0:T(4,128)S(1)}, f32[3,3,64]{2,1,0:T(4,128)}, u32[]{:S(2)}) copy-start(f32[3,3,64]{2,1,0:T(4,128)} %param.20) | copy-start | bytes 6916

commit v4 on v3

--- a/solution.py
+++ b/solution.py
@@ -281,7 +281,8 @@
         return jnp.where(lane >= LANES - k, after, rolled)
 
     def tap(i, k):
-        tile = taps_ref[3 * i + k]
+        at = 3 * i + k
+        tile = jnp.broadcast_to(taps_ref[:, at : at + 1], (8, LANES))
         return jnp.broadcast_to(tile[None], (rows // 8, 8, LANES)).reshape(rows, LANES)
 
     finish(sig_copies)
@@ -349,13 +350,16 @@
     finish(gated_copies)
     for j in range(seqs):
         unfold(gated_in[j].astype(F32), 3 * chans, j, grads)
+    share = width // seqs
+    back_out = grads[pl.ds(3 * chans, chans), :].astype(BF16)
+    w_out_buf[:, :, 3 * chans :] = (
+        (dot_rows(g_all, back_out) * scale).reshape(seqs, share, chans).astype(BF16)
+    )
     finish(pg_copies)
     for j in range(seqs):
         for i in range(3):
             unfold(pg_in[j, i].astype(F32), i * chans, j, grads)
-    back_all = grads[...].astype(BF16)
-    back_in = back_all[: 3 * chans]
-    back_out = back_all[3 * chans :]
+    back_in = grads[pl.ds(0, 3 * chans), :].astype(BF16)
 
     dx_part = lax.dot_general(
         w_turned, back_in, (((0,), (0,)), ((), ())), preferred_element_type=F32
@@ -367,11 +371,9 @@
         dx_copies.append(
             remote(dx_out.at[to], dx_in.at[mine], sems_dx.at[0, k], sems_dx.at[1, k], (me, to))
         )
-    share = width // seqs
     w_out_buf[:, :, : 3 * chans] = (dot_rows(x_all, back_in) * scale).reshape(
         seqs, share, 3 * chans
     ).astype(BF16)
-    w_out_buf[:, :, 3 * chans :] = (dot_rows(g_all, back_out) * scale).reshape(seqs, share, chans).astype(BF16)
     w_copies = exchange(w_out_buf, w_in_buf, 6)
     dx_in[mine] = dx_out[mine]
 
@@ -420,7 +422,7 @@
     me = lax.axis_index("seq")
     w_turned = w_in.transpose(0, 2, 1)
     taps = lax.dynamic_slice_in_dim(short_taps.reshape(9, chans), me * own, own, axis=1)
-    taps = jnp.broadcast_to(jnp.tile(taps, (1, 8 // own))[:, :, None], (9, 8, LANES))
+    taps = jnp.tile(taps, (1, 8 // own)).T
     tables = [jnp.asarray(table) for table in dft_tables(span * seqs, own)]
     vmem = pl.BlockSpec(memory_space=pltpu.VMEM)
     hbm = pl.BlockSpec(memory_space=pltpu.HBM)

time: 46.1 us -> 45.8 us (level)
    broadcast_in_dim x1 -> x0, local copies, waits for them, and re-layouts: 0.7 us -> none  [local(): jnp.broadcast_to(jnp.tile(taps, (1, 8 // own))[:, :, None], (9, 8, LANES))]
    unnamed x2 -> x3, local copies, waits for them, and re-layouts: 0.68 us -> 1.36 us
where the time goes in v4:
time: 45.8 us; the launch traced here: 45.6 us
  Pallas kernels  43.5 us (95%)
  local copies, waits for them, and re-layouts  1.44 us (3%)
  between operations  0.65 us (1%)
    pallas_call x1, Pallas kernels, local(): pl.pallas_call(functools.partial(kernel, seqs, groups), out_shape=(jax.Sh...  41.5 us
    pallas_call x1, Pallas kernels, local(): pl.pallas_call(closing, out_shape=(jax.ShapeDtypeStruct((chans, span), BF...  1.96 us
    unnamed x3, local copies, waits for them, and re-layouts  1.36 us

profile of v4, /device:TPU:0, one launch (start us, length us, event | category | flops | bytes accessed | tf_op | source)
XLA Modules:
  0.0 45.6 jit_solution(6919078885269056399)
XLA Ops:
  0.6 0.0 copy-start
  0.6 0.7 %copy-done = f32[3,3,64]{2,1,0:T(4,128)S(1)} copy-done((f32[3,3,64]{2,1,0:T(4,128)S(1)}, f32[3,3,64]{2,1,0:T(4,128)}, u32[]{:S(2)}) %copy-start) | copy-done | bytes 2328
  1.3 0.1 constant_dynamic-slice_fusion
  1.4 0.7 %copy.25 = f32[9,8]{0,1:T(8,128)} copy(f32[9,8]{1,0:T(8,128)S(1)} %constant_dynamic-slice_fusion) | data formatting | bytes 576
  2.1 41.5 %shard_map.208 = (bf16[8,32,256]{2,1,0:T(8,128)(2,1)}, f32[8,8,128]{2,1,0:T(8,128)}, bf16[2,8,32,128]{3,2,1,0:T(8,128)(2,1)}, f32[4,64,512]{2,1,0:T(8,128)}) custom-call(bf16[64,512]{1,0:T(8,128)(2,1)} %x_ref.1, bf16[64,512]{1,0:T(8,128)(2,1)} %g_ref.1, f32[64,512]{1,0:T(8,128)} %f1_ref.1, f32[64,512]{1,0:T(8,128)} %f2_ref.1, bf16[3,64,256]{2,1,0:T(8,128)(2,1)} %bitcast.3, ...), custom_call_target="tpu_custom_call" | custom-call | tf_op jit(solution)/shard_map/pallas_call | solution.py:429
  43.6 2.0 %shard_map.209 = (bf16[64,512]{1,0:T(8,128)(2,1)}, f32[3,32,64]{2,1,0:T(8,128)}, f32[3,3,64]{2,1,0:T(4,128)}, f32[64,512]{1,0:T(8,128)}, f32[64,512]{1,0:T(8,128)}, /*index=5*/f32[32,64]{1,0:T(8,128)}) custom-call(bf16[8,32,256]{2,1,0:T(8,128)(2,1)} %get-tuple-element.16.w_ref, f32[8,8,128]{2,1,0:T(8,128)} %get-tuple-element.17.dt_ref, ...), custom_call_target="tpu_custom_call" | custom-call | tf_op jit(solution)/shard_map/pallas_call | solution.py:470
  (1 shorter events, 0.0 us)
Async XLA Ops:
  0.6 0.7 %copy-start = (f32[3,3,64]{2,1,0:T(4,128)S(1)}, f32[3,3,64]{2,1,0:T(4,128)}, u32[]{:S(2)}) copy-start(f32[3,3,64]{2,1,0:T(4,128)} %param.20) | copy-start | bytes 6916
